TPU v7x, 256 devices: a whole 4x4x8 slice. The times are simulated.
256 devices in a mesh: dp: 4 (over x), vocab: 64 (over z, y, core).
Axes of the slice: x: 4, y: 4, z: 8, core: 2. Of those that a mesh axis runs over, the one named last changes fastest.
Arguments:
- hidden: bfloat16 [2048, 3072], P(('dp', 'vocab')), parts along dimension 0, may hold values from -60 to 60
- weight: bfloat16 [3072, 65536], P(None, 'vocab'), may hold values from -0.32421875 to 0.32421875
- targets: int32 [2048], P('dp'), parts along dimension 0, may hold values from 0 to 65535
Outputs:
- loss: float32 [4], P('dp'), parts along dimension 0
- d_hidden: bfloat16 [2048, 3072], P(('dp', 'vocab')), parts along dimension 0
- d_weight: bfloat16 [12288, 65536], P('dp', 'vocab'), parts along dimension 0
There are 4 independent parts, one for each index of `dp`. A program takes and returns all parts, laid end to end along the dimension named above; an argument that names none is the same for every part. Nothing has to cross between parts.
All inputs are finite; a program needn't handle non-finite values.
Results may differ from a plain program's by a relative error of at most 0.0035.
Values may be sent and summed in bfloat16 or wider, within the bound.
No kernel may reach another device: no remote copies, remote signals or barrier semaphores. Data moves between devices by JAX's collectives and lax.ppermute only.
A program may use at most 64 MiB of HBM per device.

v0:
```python
import jax
import jax.numpy as jnp
from jax import lax
from jax.experimental import pallas as pl
from jax.experimental.pallas import tpu as pltpu
from jax.sharding import Mesh
from jax.sharding import PartitionSpec as P

NEAR = ("zl", "y")
CHIPS = ("zh", "zl", "y")
VOCAB = ("zh", "zl", "y", "core")
DP_VOCAB = ("dp", "zh", "zl", "y", "core")
SWAP = [(0, 1), (1, 0)]
def to_each(value, axis):
    devices = lax.axis_size(axis)
    return lax.all_to_all(
        jnp.broadcast_to(value[None], (devices, *value.shape)), axis, 0, 0, tiled=True
    )


def swapped(value):
    return lax.ppermute(value, "core", SWAP)


def nothing_kernel(*refs):
    del refs


def after(value, first):
    return pl.pallas_call(
        nothing_kernel,
        in_specs=[pl.BlockSpec(memory_space=pl.ANY)] * 2,
        out_specs=pl.BlockSpec(memory_space=pl.ANY),
        out_shape=jax.ShapeDtypeStruct(value.shape, value.dtype),
        input_output_aliases={0: 0},
        compiler_params=pltpu.CompilerParams(vmem_limit_bytes=1024 * 1024),
        cost_estimate=pl.CostEstimate(flops=0, bytes_accessed=0, transcendentals=0),
    )(value, first)


def back(grads, columns):
    return lax.dot_general(
        grads, columns, (((1,), (1,)), ((), ())), preferred_element_type=jnp.float32
    )


def body(hidden, weight, targets):
    rows, depth = hidden.shape
    width = weight.shape[1]
    far, near, ys = lax.axis_size("zh"), lax.axis_size(NEAR), lax.axis_size("y")
    core = lax.axis_index("core")
    tokens = far * near * rows

    other_weight = swapped(weight)
    weights = [weight, other_weight]
    line = after(to_each(hidden, "zh"), other_weight[:16, :128])
    mine = to_each(line, NEAR).reshape(tokens, depth)
    theirs = swapped(mine)

    wanted = targets.reshape(far, near, 2, rows)
    wanted = lax.dynamic_index_in_dim(wanted, core, 2, keepdims=False)
    wanted = jnp.swapaxes(wanted, 0, 1).reshape(tokens)
    chip = lax.axis_index(CHIPS) * 2
    lanes = lax.broadcasted_iota(jnp.int32, (1, width), 1)
    hits = [(chip + at) * width + lanes == wanted[:, None] for at in (core, 1 - core)]
    target = sum(back(h.astype(jnp.bfloat16), w) for h, w in zip(hits, weights))
    target = lax.optimization_barrier(target.astype(jnp.bfloat16))

    logits = [jnp.dot(mine, w, preferred_element_type=jnp.float32) for w in weights]
    local_top = jnp.maximum(jnp.max(logits[0], axis=1), jnp.max(logits[1], axis=1))
    expo = [jnp.exp(x - local_top[:, None]) for x in logits]
    local_total = jnp.sum(expo[0], axis=1) + jnp.sum(expo[1], axis=1)
    local_picked = sum(jnp.sum(jnp.where(h, x, 0.0), axis=1) for h, x in zip(hits, logits))
    packed = jnp.stack([local_top, local_total, local_picked])
    stats = to_each(packed, CHIPS)

    local_top = after(packed, packed[1:2])[0]
    expo = [jnp.exp(x - local_top[:, None]) for x in logits]
    rest = [jnp.where(h, 0.0, e).astype(jnp.bfloat16) for h, e in zip(hits, expo)]
    others = lax.optimization_barrier(back(rest[0], weights[0]) + back(rest[1], weights[1]))

    top = jnp.max(stats[:, 0], axis=0)
    total = jnp.sum(stats[:, 1] * jnp.exp(stats[:, 0] - top[None]), axis=0)
    picked = jnp.sum(stats[:, 2], axis=0)
    factor = jnp.exp(local_top - top) / total
    at_target = (jnp.exp(picked - top) / total - 1.0).astype(jnp.bfloat16).astype(jnp.float32)
    partial = others * factor[:, None] + at_target[:, None] * target.astype(jnp.float32)
    partial = partial.astype(jnp.bfloat16).reshape(near, far, rows, depth)
    summed = lax.all_to_all(partial, NEAR, 0, 0, tiled=True)
    summed = jnp.sum(summed.astype(jnp.float32), axis=0)

    first_grad, second_grad = (
        (jnp.exp(x - top[:, None]) / total[:, None] - h.astype(jnp.float32)).astype(jnp.bfloat16)
        for x, h in zip(logits, hits)
    )
    both = jnp.concatenate([mine, theirs], axis=0)
    own = jnp.concatenate([first_grad, swapped(second_grad)], axis=0)
    d_weight = lax.dot_general(
        both, own, (((0,), (0,)), ((), ())), preferred_element_type=jnp.float32
    ).astype(jnp.bfloat16)

    summed = lax.all_to_all(after(summed, d_weight[:16, :128]), "zh", 0, 0, tiled=True)
    d_hidden = jnp.sum(summed, axis=0).astype(jnp.bfloat16)

    part = jnp.sum(top + jnp.log(total) - picked).reshape(1)
    loss = (part + swapped(part)) / (2 * tokens)
    return (loss, d_hidden, d_weight)


def solution(mesh):
    torus = Mesh(mesh.devices.reshape(mesh.shape["dp"], 4, 2, 4, 2), DP_VOCAB)
    return jax.shard_map(
        body,
        mesh=torus,
        in_specs=(P(DP_VOCAB, None), P(None, VOCAB), P("dp")),
        out_specs=(P("dp"), P(DP_VOCAB, None), P("dp", VOCAB)),
        check_vma=False,
    )
```

profile of v0, /device:TPU:4, one launch (start us, length us, event | category | flops | bytes accessed | tf_op | source)
XLA Modules:
  0.0 124.6 jit_solution(9805204091922069680)
XLA Ops:
  0.6 0.0 copy-start.6
  0.6 0.1 collective-permute-start
  0.7 1.5 %broadcast_in_dim.13 = bf16[4,8,3072]{2,1,0:T(8,128)(2,1)} broadcast(bf16[8,3072]{1,0:T(8,128)(2,1)} %param.3), dimensions={1,2} | broadcast | bytes 245760 | tf_op jit(solution)/shard_map/broadcast_in_dim | solution.py:17
  2.2 8.5 %all-to-all-start = ((bf16[4,8,3072]{2,1,0:T(8,128)(2,1)}), bf16[4,8,3072]{2,1,0:T(8,128)(2,1)S(1)}, u32[]{:S(2)}, u32[]{:S(2)}) async-start(bf16[4,8,3072]{2,1,0:T(8,128)(2,1)} %broadcast_in_dim.13), calls=%async_computation | async-start | bytes 393216 | tf_op jit(solution)/shard_map/all_to_all | solution.py:16
  10.7 0.5 collective-permute-done
  11.2 0.7 slice.25.refs_1_
  11.9 8.9 %all-to-all-done.refs_0_ = bf16[4,8,3072]{2,1,0:T(8,128)(2,1)S(1)} async-done(((bf16[4,8,3072]{2,1,0:T(8,128)(2,1)}), bf16[4,8,3072]{2,1,0:T(8,128)(2,1)S(1)}, u32[]{:S(2)}, u32[]{:S(2)}) %all-to-all-start) | async-done | bytes 196640 | tf_op jit(solution)/shard_map/all_to_all | solution.py:16
  20.8 1.3 %broadcast_in_dim.14 = bf16[8,4,8,3072]{3,2,1,0:T(8,128)(2,1)} broadcast(bf16[4,8,3072]{2,1,0:T(8,128)(2,1)S(1)} %shard_map.58), dimensions={1,2,3} | broadcast | bytes 1769472 | tf_op jit(solution)/shard_map/broadcast_in_dim | solution.py:17
  22.1 4.9 %all-to-all-start.1 = ((bf16[8,4,8,3072]{3,2,1,0:T(8,128)(2,1)}), bf16[8,4,8,3072]{3,2,1,0:T(8,128)(2,1)S(1)}, u32[]{:S(2)}, u32[]{:S(2)}) async-start(bf16[8,4,8,3072]{3,2,1,0:T(8,128)(2,1)} %broadcast_in_dim.14), calls=%async_computation.1 | async-start | bytes 3145728 | tf_op jit(solution)/shard_map/all_to_all | solution.py:16
  27.0 0.0 copy-done.6
  27.0 0.1 reshape.101
  27.2 0.1 eq.13
  27.3 4.6 %fusion.5 = f32[256,3072]{1,0:T(8,128)S(1)} fusion(bf16[3072,1024]{1,0:T(8,128)(2,1)} %param.4, s32[1024]{0:T(1024)S(1)} %get-tuple-element.23, s32[256]{0:T(256)S(1)} %eq.13), kind=kOutput, calls=%fused_computation.14 | convolution fusion | flops 1610874880 | bytes 9442304 | tf_op jit(solution)/shard_map/dot_general | solution.py:42
  31.9 5.8 %fusion = bf16[256,3072]{1,0:T(8,128)(2,1)} fusion(f32[256,3072]{1,0:T(8,128)S(1)} %fusion.5, bf16[3072,1024]{1,0:T(8,128)(2,1)} %collective-permute-done, s32[1024]{0:T(1024)S(1)} %get-tuple-element.22, s32[256]{0:T(256)S(1)} %eq.13), kind=kOutput, calls=%fused_computation.3 | convolution fusion | flops 1612447744 | bytes 11015168 | tf_op jit(solution)/shard_map/dot_general | solution.py:42
  37.8 8.7 %all-to-all-done.1 = bf16[8,4,8,3072]{3,2,1,0:T(8,128)(2,1)S(1)} async-done(((bf16[8,4,8,3072]{3,2,1,0:T(8,128)(2,1)}), bf16[8,4,8,3072]{3,2,1,0:T(8,128)(2,1)S(1)}, u32[]{:S(2)}, u32[]{:S(2)}) %all-to-all-start.1) | async-done | bytes 1572896 | tf_op jit(solution)/shard_map/all_to_all | solution.py:16
  46.5 5.2 %fusion.41 = (f32[256]{0:T(256)S(1)}, f32[256,1024]{1,0:T(8,128)S(1)}) fusion(bf16[256,3072]{1,0:T(8,128)(2,1)S(1)} %bitcast.33, bf16[3072,1024]{1,0:T(8,128)(2,1)} %param.4), kind=kOutput, calls=%fused_computation.63 | convolution fusion | flops 1610874624 | bytes 8913920 | tf_op jit(solution)/shard_map/dot_general | solution.py:69
  51.7 0.0 copy-done.4
  51.7 0.0 copy-start.3
  51.7 5.0 %fusion.42 = (f32[256]{0:T(256)S(1)}, f32[256,1024]{1,0:T(8,128)S(1)}) fusion(bf16[256,3072]{1,0:T(8,128)(2,1)S(1)} %bitcast.34, bf16[3072,1024]{1,0:T(8,128)(2,1)} %collective-permute-done), kind=kOutput, calls=%fused_computation.64 | convolution fusion | flops 1610874624 | bytes 8913920 | tf_op jit(solution)/shard_map/dot_general | solution.py:69
  56.8 0.7 exponential_reduce_fusion.1
  57.5 0.3 copy-done
  57.8 0.7 broadcast_in_dim.16
  58.5 5.1 %all-to-all-start.2 = ((f32[32,3,256]{2,1,0:T(4,128)}), f32[32,3,256]{2,1,0:T(4,128)S(1)}, u32[]{:S(2)}, u32[]{:S(2)}) async-start(f32[32,3,256]{2,1,0:T(4,128)} %broadcast_in_dim.16), calls=%async_computation.2 | async-start | bytes 262144 | tf_op jit(solution)/shard_map/all_to_all | solution.py:16
  63.6 0.0 copy-done.3
  63.6 0.0 copy-start.1
  63.6 4.8 %fusion.19 = f32[256,3072]{1,0:T(8,128)S(1)} fusion(bf16[3072,1024]{1,0:T(8,128)(2,1)} %param.4, f32[256,1024]{1,0:T(8,128)S(1)} %get-tuple-element.19, f32[256]{0:T(256)S(1)} %bitcast.38, s32[1024]{0:T(1024)S(1)} %get-tuple-element.23, s32[256]{0:T(256)S(1)} %eq.13), kind=kOutput, calls=%fused_computation.31 | convolution fusion | flops 1611661312 | bytes 10491904 | tf_op jit(solution)/shard_map/dot_general | solution.py:42
  68.4 4.8 %convolution_add_fusion = f32[256,3072]{1,0:T(8,128)S(1)} fusion(f32[256,3072]{1,0:T(8,128)S(1)} %fusion.19, bf16[3072,1024]{1,0:T(8,128)(2,1)} %collective-permute-done, f32[256,1024]{1,0:T(8,128)S(1)} %copy-done.1, f32[256]{0:T(256)S(1)} %bitcast.39, s32[1024]{0:T(1024)S(1)} %get-tuple-element.22, s32[256]{0:T(256)S(1)} %eq.13), kind=kOutput, calls=%fused_computation.1 | convolution fusion | flops 1612447744 | bytes 13637632 | tf_op jit(solution)/shard_map/dot_general | solution.py:42
  73.2 0.9 all-to-all-done.2
  74.1 0.1 slice_reduce_fusion.1
  74.2 0.6 fusion.37
  74.8 3.3 %add_convert_fusion = bf16[256,3072]{1,0:T(8,128)(2,1)} fusion(bf16[256,3072]{1,0:T(8,128)(2,1)} %fusion, f32[256,3072]{1,0:T(8,128)S(1)} %convolution_add_fusion, f32[256]{0:T(256)S(1)} %get-tuple-element.15, f32[256]{0:T(256)S(1)} %get-tuple-element.17), kind=kLoop, calls=%fused_computation.8 | loop fusion | flops 3932160 | bytes 6293504 | tf_op jit(solution)/shard_map/convert_element_type | solution.py:88
  78.1 4.6 %all-to-all-start.3 = ((bf16[8,4,8,3072]{3,2,1,0:T(8,128)(2,1)}), bf16[8,4,8,3072]{3,2,1,0:T(8,128)(2,1)S(1)}, u32[]{:S(2)}, u32[]{:S(2)}) async-start(bf16[8,4,8,3072]{3,2,1,0:T(8,128)(2,1)} %bitcast.32), calls=%async_computation.3 | async-start | bytes 3145728 | tf_op jit(solution)/shard_map/all_to_all | solution.py:89
  82.6 0.1 collective-permute-start.2
  82.8 1.9 %fusion.10 = (bf16[256,1024]{1,0:T(8,128)(2,1)S(1)}, bf16[256,1024]{1,0:T(8,128)(2,1)S(1)}) fusion(f32[256,1024]{1,0:T(8,128)} %copy-done.3, f32[256]{0:T(256)S(1)} %fusion.36, f32[256]{0:T(256)S(1)} %get-tuple-element.7, s32[1024]{0:T(1024)S(1)} %get-tuple-element.23, s32[256]{0:T(256)S(1)} %eq.13, s32[1024]{0:T(1024)S(1)} %get-tuple-element.22, ...), kind=kLoop, calls=%fused_computation.21 | loop fusion | flops 3145728 | bytes 3156992 | tf_op jit(solution)/shard_map/convert_element_type | solution.py:93
  84.7 0.5 collective-permute-start.3
  85.2 1.7 %collective-permute-done.3 = bf16[256,1024]{1,0:T(8,128)(2,1)S(1)} collective-permute-done((bf16[256,1024]{1,0:T(8,128)(2,1)S(1)}, bf16[256,1024]{1,0:T(8,128)(2,1)S(1)}, u32[]{:S(2)}, u32[]{:S(2)}) %collective-permute-start.3) | collective-permute-done | bytes 524320 | tf_op jit(solution)/shard_map/ppermute | solution.py:22
  86.9 0.0 collective-permute-done.2
  86.9 0.0 copy-done.5
  86.9 3.7 %convolution_convert_fusion = bf16[3072,1024]{1,0:T(8,128)(2,1)S(1)} fusion(bf16[256,3072]{1,0:T(8,128)(2,1)S(1)} %collective-permute-done.2, bf16[256,3072]{1,0:T(8,128)(2,1)S(1)} %bitcast.36, bf16[256,1024]{1,0:T(8,128)(2,1)S(1)} %collective-permute-done.3, bf16[256,1024]{1,0:T(8,128)(2,1)S(1)} %get-tuple-element.13), kind=kOutput, calls=%fused_computation | convolution fusion | flops 3232759808 | bytes 10485760 | tf_op jit(solution)/shard_map/dot_general | solution.py:98
  90.6 0.0 copy-start.7
  90.6 2.7 %copy-done.7 = bf16[3072,1024]{1,0:T(8,128)(2,1)} copy-done((bf16[3072,1024]{1,0:T(8,128)(2,1)}, bf16[3072,1024]{1,0:T(8,128)(2,1)S(1)}, u32[]{:S(2)}) %copy-start.7) | copy-done | bytes 6291480
  93.3 9.4 %all-to-all-done.3 = bf16[8,4,8,3072]{3,2,1,0:T(8,128)(2,1)S(1)} async-done(((bf16[8,4,8,3072]{3,2,1,0:T(8,128)(2,1)}), bf16[8,4,8,3072]{3,2,1,0:T(8,128)(2,1)S(1)}, u32[]{:S(2)}, u32[]{:S(2)}) %all-to-all-start.3) | async-done | bytes 1572896 | tf_op jit(solution)/shard_map/all_to_all | solution.py:89
  102.7 1.0 convert_reduce_fusion.refs_0_
  103.6 5.8 %all-to-all-start.4 = ((f32[4,8,3072]{2,1,0:T(8,128)}), f32[4,8,3072]{2,1,0:T(8,128)S(1)}, u32[]{:S(2)}, u32[]{:S(2)}) async-start(f32[4,8,3072]{2,1,0:T(8,128)} %shard_map.60), calls=%async_computation.4 | async-start | bytes 786432 | tf_op jit(solution)/shard_map/all_to_all | solution.py:102
  109.4 0.0 collective-permute-start.1
  109.4 1.2 collective-permute-done.1
  111.9 10.9 %all-to-all-done.4 = f32[4,8,3072]{2,1,0:T(8,128)S(1)} async-done(((f32[4,8,3072]{2,1,0:T(8,128)}), f32[4,8,3072]{2,1,0:T(8,128)S(1)}, u32[]{:S(2)}, u32[]{:S(2)}) %all-to-all-start.4) | async-done | bytes 393248 | tf_op jit(solution)/shard_map/all_to_all | solution.py:102
  122.9 0.6 reduce_sum.89
  (19 shorter events, 0.1 us)
Async XLA Ops:
  0.6 26.4 %copy-start.6 = (s32[512]{0:T(512)S(1)}, s32[512]{0:T(512)}, u32[]{:S(2)}) copy-start(s32[512]{0:T(512)} %param.5) | copy-start | bytes 6148
  0.6 10.6 %collective-permute-start = (bf16[3072,1024]{1,0:T(8,128)(2,1)}, bf16[3072,1024]{1,0:T(8,128)(2,1)}, u32[]{:S(2)}, u32[]{:S(2)}) collective-permute-start(bf16[3072,1024]{1,0:T(8,128)(2,1)} %param.4), channel_id=1, source_target_pairs={{0,1},{1,0},{2,3},{3,2},{4,5},{5,4},{6,7},{7,6},{8,9},{9,8},{10,11... | collective-permute-start | bytes 18874376 | tf_op jit(solution)/shard_map/ppermute | solution.py:22
  2.2 18.6 %all-to-all-start = ((bf16[4,8,3072]{2,1,0:T(8,128)(2,1)}), bf16[4,8,3072]{2,1,0:T(8,128)(2,1)S(1)}, u32[]{:S(2)}, u32[]{:S(2)}) async-start(bf16[4,8,3072]{2,1,0:T(8,128)(2,1)} %broadcast_in_dim.13), calls=%async_computation | async-start | bytes 393216 | tf_op jit(solution)/shard_map/all_to_all | solution.py:16
  22.1 24.4 %all-to-all-start.1 = ((bf16[8,4,8,3072]{3,2,1,0:T(8,128)(2,1)}), bf16[8,4,8,3072]{3,2,1,0:T(8,128)(2,1)S(1)}, u32[]{:S(2)}, u32[]{:S(2)}) async-start(bf16[8,4,8,3072]{3,2,1,0:T(8,128)(2,1)} %broadcast_in_dim.14), calls=%async_computation.1 | async-start | bytes 3145728 | tf_op jit(solution)/shard_map/all_to_all | solution.py:16
  46.5 5.2 %copy-start.4 = (bf16[8,4,8,3072]{3,2,1,0:T(8,128)(2,1)}, bf16[8,4,8,3072]{3,2,1,0:T(8,128)(2,1)S(1)}, u32[]{:S(2)}) copy-start(bf16[8,4,8,3072]{3,2,1,0:T(8,128)(2,1)S(1)} %all-to-all-done.1) | copy-start | bytes 4718596
  51.7 11.9 %copy-start.3 = (f32[256,1024]{1,0:T(8,128)}, f32[256,1024]{1,0:T(8,128)S(1)}, u32[]{:S(2)}) copy-start(f32[256,1024]{1,0:T(8,128)S(1)} %get-tuple-element.19) | copy-start | bytes 3145732
  56.8 1.0 copy-start
  58.5 15.6 %all-to-all-start.2 = ((f32[32,3,256]{2,1,0:T(4,128)}), f32[32,3,256]{2,1,0:T(4,128)S(1)}, u32[]{:S(2)}, u32[]{:S(2)}) async-start(f32[32,3,256]{2,1,0:T(4,128)} %broadcast_in_dim.16), calls=%async_computation.2 | async-start | bytes 262144 | tf_op jit(solution)/shard_map/all_to_all | solution.py:16
  63.6 4.8 %copy-start.1 = (f32[256,1024]{1,0:T(8,128)S(1)}, f32[256,1024]{1,0:T(8,128)}, u32[]{:S(2)}) copy-start(f32[256,1024]{1,0:T(8,128)} %copy-done) | copy-start | bytes 3145732
  78.1 4.7 %copy-start.2 = (f32[256,1024]{1,0:T(8,128)S(1)}, f32[256,1024]{1,0:T(8,128)}, u32[]{:S(2)}) copy-start(f32[256,1024]{1,0:T(8,128)} %copy-done) | copy-start | bytes 3145732
  78.1 24.6 %all-to-all-start.3 = ((bf16[8,4,8,3072]{3,2,1,0:T(8,128)(2,1)}), bf16[8,4,8,3072]{3,2,1,0:T(8,128)(2,1)S(1)}, u32[]{:S(2)}, u32[]{:S(2)}) async-start(bf16[8,4,8,3072]{3,2,1,0:T(8,128)(2,1)} %bitcast.32), calls=%async_computation.3 | async-start | bytes 3145728 | tf_op jit(solution)/shard_map/all_to_all | solution.py:89
  82.6 4.3 %copy-start.5 = (bf16[8,4,8,3072]{3,2,1,0:T(8,128)(2,1)S(1)}, bf16[8,4,8,3072]{3,2,1,0:T(8,128)(2,1)}, u32[]{:S(2)}) copy-start(bf16[8,4,8,3072]{3,2,1,0:T(8,128)(2,1)} %copy-done.4) | copy-start | bytes 4718596
  82.6 4.2 %collective-permute-start.2 = (bf16[256,3072]{1,0:T(8,128)(2,1)}, bf16[256,3072]{1,0:T(8,128)(2,1)S(1)}, u32[]{:S(2)}, u32[]{:S(2)}) collective-permute-start(bf16[256,3072]{1,0:T(8,128)(2,1)} %bitcast.35), channel_id=1, source_target_pairs={{0,1},{1,0},{2,3},{3,2},{4,5},{5,4},{6,7},{7,6},{8,9},{9,8},{10,11... | collective-permute-start | bytes 4718600 | tf_op jit(solution)/shard_map/ppermute | solution.py:22
  84.7 2.2 %collective-permute-start.3 = (bf16[256,1024]{1,0:T(8,128)(2,1)S(1)}, bf16[256,1024]{1,0:T(8,128)(2,1)S(1)}, u32[]{:S(2)}, u32[]{:S(2)}) collective-permute-start(bf16[256,1024]{1,0:T(8,128)(2,1)S(1)} %get-tuple-element.14), channel_id=1, source_target_pairs={{0,1},{1,0},{2,3},{3,2},{4,5},{5,4},{6,7},{7,6},{8,9},{9,8},{10,11... | collective-permute-start | bytes 1572872 | tf_op jit(solution)/shard_map/ppermute | solution.py:22
  90.6 2.7 %copy-start.7 = (bf16[3072,1024]{1,0:T(8,128)(2,1)}, bf16[3072,1024]{1,0:T(8,128)(2,1)S(1)}, u32[]{:S(2)}) copy-start(bf16[3072,1024]{1,0:T(8,128)(2,1)S(1)} %convolution_convert_fusion) | copy-start | bytes 18874372
  103.6 19.2 %all-to-all-start.4 = ((f32[4,8,3072]{2,1,0:T(8,128)}), f32[4,8,3072]{2,1,0:T(8,128)S(1)}, u32[]{:S(2)}, u32[]{:S(2)}) async-start(f32[4,8,3072]{2,1,0:T(8,128)} %shard_map.60), calls=%async_computation.4 | async-start | bytes 786432 | tf_op jit(solution)/shard_map/all_to_all | solution.py:102
  109.4 1.2 collective-permute-start.1
where the time goes:
time: 125 us
  waiting for transfers between devices  42.3 us (34%)
  matrix products  33.9 us (27%)
  starting transfers between devices  29.5 us (24%)
  other arithmetic  8.23 us (7%)
  local copies, waits for them, and re-layouts  7.43 us (6%)
  between operations  3.28 us (3%)
    dot_general x4, matrix products, back(): lax.dot_general(grads, columns, (((1,), (1,)), ((), ())), preferred_eleme...  20 us
    all_to_all x3, waiting for transfers between devices, to_each(): lax.all_to_all(jnp.broadcast_to(value[None], (devices, *value.shape)), ax...  18.5 us
    all_to_all x3, starting transfers between devices, to_each(): lax.all_to_all(jnp.broadcast_to(value[None], (devices, *value.shape)), ax...  18.5 us
    all_to_all x1, waiting for transfers between devices, body(): lax.all_to_all(after(summed, d_weight[:16, :128]), 'zh', 0, 0, tiled=True)  10.9 us
    dot_general x2, matrix products, body(): jnp.dot(mine, w, preferred_element_type=jnp.float32)  10.3 us
    all_to_all x1, waiting for transfers between devices, body(): summed = lax.all_to_all(partial, NEAR, 0, 0, tiled=True)  9.35 us
    all_to_all x1, starting transfers between devices, body(): lax.all_to_all(after(summed, d_weight[:16, :128]), 'zh', 0, 0, tiled=True)  5.77 us
    all_to_all x1, starting transfers between devices, body(): summed = lax.all_to_all(partial, NEAR, 0, 0, tiled=True)  4.56 us
  transfers between devices with their start and end apart: 9, of which 8 were waited for; matrix products, arithmetic and copies ran while one was open for 22% of the time, Pallas kernels for 0%

commit v1 on v0

--- a/solution.py
+++ b/solution.py
@@ -18,6 +18,16 @@
     )
 
 
+def from_each(value, axis):
+    n, me = lax.axis_size(axis), lax.axis_index(axis)
+    shifts = sorted(range(1, n), key=lambda k: -min(k, n - k))
+    pieces = [(k, lax.ppermute(value, axis, [(i, (i + k) % n) for i in range(n)])) for k in shifts]
+    found = jnp.zeros((n, *value.shape), value.dtype)
+    for k, piece in [(0, value)] + pieces:
+        found = lax.dynamic_update_index_in_dim(found, piece, lax.rem(me - k + n, n), 0)
+    return found
+
+
 def swapped(value):
     return lax.ppermute(value, "core", SWAP)
 
@@ -26,10 +36,12 @@
     del refs
 
 
-def after(value, first):
+def after(value, first, space=pltpu.HBM):
+    if space != pl.ANY:
+        first = pltpu.with_memory_space_constraint(first, space)
     return pl.pallas_call(
         nothing_kernel,
-        in_specs=[pl.BlockSpec(memory_space=pl.ANY)] * 2,
+        in_specs=[pl.BlockSpec(memory_space=m) for m in (pl.ANY, space)],
         out_specs=pl.BlockSpec(memory_space=pl.ANY),
         out_shape=jax.ShapeDtypeStruct(value.shape, value.dtype),
         input_output_aliases={0: 0},
@@ -53,7 +65,7 @@
 
     other_weight = swapped(weight)
     weights = [weight, other_weight]
-    line = after(to_each(hidden, "zh"), other_weight[:16, :128])
+    line = after(from_each(hidden, "zh"), other_weight)
     mine = to_each(line, NEAR).reshape(tokens, depth)
     theirs = swapped(mine)
 
@@ -74,7 +86,7 @@
     packed = jnp.stack([local_top, local_total, local_picked])
     stats = to_each(packed, CHIPS)
 
-    local_top = after(packed, packed[1:2])[0]
+    local_top = after(packed, packed[1:2], pl.ANY)[0]
     expo = [jnp.exp(x - local_top[:, None]) for x in logits]
     rest = [jnp.where(h, 0.0, e).astype(jnp.bfloat16) for h, e in zip(hits, expo)]
     others = lax.optimization_barrier(back(rest[0], weights[0]) + back(rest[1], weights[1]))
@@ -99,7 +111,7 @@
         both, own, (((0,), (0,)), ((), ())), preferred_element_type=jnp.float32
     ).astype(jnp.bfloat16)
 
-    summed = lax.all_to_all(after(summed, d_weight[:16, :128]), "zh", 0, 0, tiled=True)
+    summed = lax.all_to_all(after(summed, d_weight), "zh", 0, 0, tiled=True)
     d_hidden = jnp.sum(summed, axis=0).astype(jnp.bfloat16)
 
     part = jnp.sum(top + jnp.log(total) - picked).reshape(1)

time: 125 us -> 122 us (0.976)
  waiting for transfers between devices: 42.3 us -> 34.5 us
  starting transfers between devices: 29.5 us -> 36.1 us
  local copies, waits for them, and re-layouts: 7.43 us -> 3.41 us
  matrix products: 33.9 us -> 35.6 us
    ppermute x0 -> x3, starting transfers between devices: none -> 11.4 us  [from_each(): lax.ppermute(value, axis, [(i, (i + k) % n) for i in range(n)])]
    all_to_all x3 -> x2, waiting for transfers between devices: 18.5 us -> 8.88 us  [to_each(): lax.all_to_all(jnp.broadcast_to(value[None], (devices, *value.shape)), ax...]
    all_to_all x3 -> x2, starting transfers between devices: 18.5 us -> 13.6 us  [to_each(): lax.all_to_all(jnp.broadcast_to(value[None], (devices, *value.shape)), ax...]
    unnamed x16 -> x14, local copies, waits for them, and re-layouts: 3.05 us -> 0.35 us
    ppermute x0 -> x3, waiting for transfers between devices: none -> 1.78 us  [from_each(): lax.ppermute(value, axis, [(i, (i + k) % n) for i in range(n)])]
    dot_general x1, matrix products: 3.71 us -> 5.37 us  [body(): lax.dot_general(both, own, (((0,), (0,)), ((), ())), preferred_element_ty...]
    broadcast_in_dim x3 -> x2, local copies, waits for them, and re-layouts: 3.47 us -> 1.99 us  [to_each(): jnp.broadcast_to(value[None], (devices, *value.shape))]
  transfers between devices with their start and end apart: 9 -> 11, of which waited for: 8 -> 8; matrix products, arithmetic and copies ran while one was open for 22% -> 23% of each run, Pallas kernels for 0% -> 0%
where the time goes in v1:
time: 122 us; the launch traced here: 121 us
  starting transfers between devices  36.1 us (30%)
  matrix products  35.6 us (29%)
  waiting for transfers between devices  34.5 us (28%)
  other arithmetic  8.23 us (7%)
  local copies, waits for them, and re-layouts  3.41 us (3%)
  between operations  3.28 us (3%)
    dot_general x4, matrix products, back(): lax.dot_general(grads, columns, (((1,), (1,)), ((), ())), preferred_eleme...  20 us
    all_to_all x2, starting transfers between devices, to_each(): lax.all_to_all(jnp.broadcast_to(value[None], (devices, *value.shape)), ax...  13.6 us
    ppermute x3, starting transfers between devices, from_each(): lax.ppermute(value, axis, [(i, (i + k) % n) for i in range(n)])  11.4 us
    all_to_all x1, waiting for transfers between devices, body(): summed = lax.all_to_all(after(summed, d_weight), 'zh', 0, 0, tiled=True)  10.9 us
    dot_general x2, matrix products, body(): jnp.dot(mine, w, preferred_element_type=jnp.float32)  10.3 us
    all_to_all x1, waiting for transfers between devices, body(): summed = lax.all_to_all(partial, NEAR, 0, 0, tiled=True)  9.97 us
    all_to_all x2, waiting for transfers between devices, to_each(): lax.all_to_all(jnp.broadcast_to(value[None], (devices, *value.shape)), ax...  8.88 us
    all_to_all x1, starting transfers between devices, body(): summed = lax.all_to_all(after(summed, d_weight), 'zh', 0, 0, tiled=True)  5.77 us
  transfers between devices with their start and end apart: 11, of which 8 were waited for; matrix products, arithmetic and copies ran while one was open for 23% of the time, Pallas kernels for 0%

profile of v1, /device:TPU:4, one launch (start us, length us, event | category | flops | bytes accessed | tf_op | source)
XLA Modules:
  0.0 121.2 jit_solution(9455595273889527003)
XLA Ops:
  0.6 0.1 collective-permute-start.3
  0.7 7.3 %collective-permute-start = (bf16[8,3072]{1,0:T(8,128)(2,1)}, bf16[8,3072]{1,0:T(8,128)(2,1)S(1)}, u32[]{:S(2)}, u32[]{:S(2)}) collective-permute-start(bf16[8,3072]{1,0:T(8,128)(2,1)} %param.3), channel_id=1, source_target_pairs={{0,32},{16,48},{32,0},{48,16},{1,33},{17,49},{33,1},{49,17},{2,34}... | collective-permute-start | bytes 147464 | tf_op jit(solution)/shard_map/ppermute | solution.py:24
  8.0 1.5 %collective-permute-start.1 = (bf16[8,3072]{1,0:T(8,128)(2,1)}, bf16[8,3072]{1,0:T(8,128)(2,1)S(1)}, u32[]{:S(2)}, u32[]{:S(2)}) collective-permute-start(bf16[8,3072]{1,0:T(8,128)(2,1)} %param.3), channel_id=1, source_target_pairs={{0,16},{16,32},{32,48},{48,0},{1,17},{17,33},{33,49},{49,1},{2,18}... | collective-permute-start | bytes 147464 | tf_op jit(solution)/shard_map/ppermute | solution.py:24
  9.5 2.7 %collective-permute-start.2 = (bf16[8,3072]{1,0:T(8,128)(2,1)}, bf16[8,3072]{1,0:T(8,128)(2,1)S(1)}, u32[]{:S(2)}, u32[]{:S(2)}) collective-permute-start(bf16[8,3072]{1,0:T(8,128)(2,1)} %param.3), channel_id=1, source_target_pairs={{0,48},{16,0},{32,16},{48,32},{1,49},{17,1},{33,17},{49,33},{2,50}... | collective-permute-start | bytes 147464 | tf_op jit(solution)/shard_map/ppermute | solution.py:24
  12.2 0.8 bitcast_dynamic-update-slice_fusion.3
  13.0 0.0 collective-permute-done
  13.0 1.4 %collective-permute-done.1 = bf16[8,3072]{1,0:T(8,128)(2,1)S(1)} collective-permute-done((bf16[8,3072]{1,0:T(8,128)(2,1)}, bf16[8,3072]{1,0:T(8,128)(2,1)S(1)}, u32[]{:S(2)}, u32[]{:S(2)}) %collective-permute-start.1) | collective-permute-done | bytes 49184 | tf_op jit(solution)/shard_map/ppermute | solution.py:24
  14.4 0.4 collective-permute-done.2
  14.8 0.0 collective-permute-done.3.refs_1_
  14.8 0.0 copy-start.6
  14.8 1.3 %broadcast_in_dim.50 = bf16[8,4,8,3072]{3,2,1,0:T(8,128)(2,1)} broadcast(bf16[4,8,3072]{2,1,0:T(8,128)(2,1)S(1)} %shard_map.58), dimensions={1,2,3} | broadcast | bytes 1769472 | tf_op jit(solution)/shard_map/broadcast_in_dim | solution.py:17
  16.1 5.4 %all-to-all-start = ((bf16[8,4,8,3072]{3,2,1,0:T(8,128)(2,1)}), bf16[8,4,8,3072]{3,2,1,0:T(8,128)(2,1)S(1)}, u32[]{:S(2)}, u32[]{:S(2)}) async-start(bf16[8,4,8,3072]{3,2,1,0:T(8,128)(2,1)} %broadcast_in_dim.50), calls=%async_computation | async-start | bytes 3145728 | tf_op jit(solution)/shard_map/all_to_all | solution.py:16
  21.5 0.0 copy-done.6
  21.5 0.1 reshape.100
  21.7 0.1 eq.13
  21.8 4.6 %fusion.5 = f32[256,3072]{1,0:T(8,128)S(1)} fusion(bf16[3072,1024]{1,0:T(8,128)(2,1)} %param.4, s32[1024]{0:T(1024)S(1)} %get-tuple-element.23, s32[256]{0:T(256)S(1)} %eq.13), kind=kOutput, calls=%fused_computation.14 | convolution fusion | flops 1610874880 | bytes 9442304 | tf_op jit(solution)/shard_map/dot_general | solution.py:54
  26.4 5.8 %fusion = bf16[256,3072]{1,0:T(8,128)(2,1)} fusion(f32[256,3072]{1,0:T(8,128)S(1)} %fusion.5, bf16[3072,1024]{1,0:T(8,128)(2,1)} %collective-permute-done.3.refs_1_, s32[1024]{0:T(1024)S(1)} %get-tuple-element.22, s32[256]{0:T(256)S(1)} %eq.13), kind=kOutput, calls=%fused_computation.3 | convolution fusion | flops 1612447744 | bytes 11015168 | tf_op jit(solution)/shard_map/dot_general | solution.py:54
  32.2 8.1 %all-to-all-done = bf16[8,4,8,3072]{3,2,1,0:T(8,128)(2,1)S(1)} async-done(((bf16[8,4,8,3072]{3,2,1,0:T(8,128)(2,1)}), bf16[8,4,8,3072]{3,2,1,0:T(8,128)(2,1)S(1)}, u32[]{:S(2)}, u32[]{:S(2)}) %all-to-all-start) | async-done | bytes 1572896 | tf_op jit(solution)/shard_map/all_to_all | solution.py:16
  40.3 5.2 %fusion.41 = (f32[256]{0:T(256)S(1)}, f32[256,1024]{1,0:T(8,128)S(1)}) fusion(bf16[256,3072]{1,0:T(8,128)(2,1)S(1)} %bitcast.41, bf16[3072,1024]{1,0:T(8,128)(2,1)} %param.4), kind=kOutput, calls=%fused_computation.67 | convolution fusion | flops 1610874624 | bytes 8913920 | tf_op jit(solution)/shard_map/dot_general | solution.py:81
  45.6 0.0 copy-done.4
  45.6 0.0 copy-start.3
  45.6 5.0 %fusion.42 = (f32[256]{0:T(256)S(1)}, f32[256,1024]{1,0:T(8,128)S(1)}) fusion(bf16[256,3072]{1,0:T(8,128)(2,1)S(1)} %bitcast.42, bf16[3072,1024]{1,0:T(8,128)(2,1)} %collective-permute-done.3.refs_1_), kind=kOutput, calls=%fused_computation.68 | convolution fusion | flops 1610874624 | bytes 8913920 | tf_op jit(solution)/shard_map/dot_general | solution.py:81
  50.6 0.7 exponential_reduce_fusion.1
  51.3 0.3 copy-done
  51.7 0.7 broadcast_in_dim.52
  52.3 8.2 %all-to-all-start.1 = ((f32[32,3,256]{2,1,0:T(4,128)}), f32[32,3,256]{2,1,0:T(4,128)S(1)}, u32[]{:S(2)}, u32[]{:S(2)}) async-start(f32[32,3,256]{2,1,0:T(4,128)} %broadcast_in_dim.52), calls=%async_computation.1 | async-start | bytes 262144 | tf_op jit(solution)/shard_map/all_to_all | solution.py:16
  60.6 0.0 copy-done.3
  60.6 0.0 copy-start.1
  60.6 4.8 %fusion.19 = f32[256,3072]{1,0:T(8,128)S(1)} fusion(bf16[3072,1024]{1,0:T(8,128)(2,1)} %param.4, f32[256,1024]{1,0:T(8,128)S(1)} %get-tuple-element.19, f32[256]{0:T(256)S(1)} %bitcast.46, s32[1024]{0:T(1024)S(1)} %get-tuple-element.23, s32[256]{0:T(256)S(1)} %eq.13), kind=kOutput, calls=%fused_computation.31 | convolution fusion | flops 1611661312 | bytes 10491904 | tf_op jit(solution)/shard_map/dot_general | solution.py:54
  65.4 4.8 %convolution_add_fusion = f32[256,3072]{1,0:T(8,128)S(1)} fusion(f32[256,3072]{1,0:T(8,128)S(1)} %fusion.19, bf16[3072,1024]{1,0:T(8,128)(2,1)} %collective-permute-done.3.refs_1_, f32[256,1024]{1,0:T(8,128)S(1)} %copy-done.1, f32[256]{0:T(256)S(1)} %bitcast.47, s32[1024]{0:T(1024)S(1)} %get-tuple-element.22, s32[256]{0:T(256)S(1)} %eq.13), kind=kOutput, calls=%fused_computation.1 | convolution fusion | flops 1612447744 | bytes 13637632 | tf_op jit(solution)/shard_map/dot_general | solution.py:54
  70.2 0.8 all-to-all-done.1
  70.9 0.1 slice_reduce_fusion.1
  71.1 0.6 fusion.37
  71.7 3.3 %add_convert_fusion = bf16[256,3072]{1,0:T(8,128)(2,1)} fusion(bf16[256,3072]{1,0:T(8,128)(2,1)} %fusion, f32[256,3072]{1,0:T(8,128)S(1)} %convolution_add_fusion, f32[256]{0:T(256)S(1)} %get-tuple-element.15, f32[256]{0:T(256)S(1)} %get-tuple-element.17), kind=kLoop, calls=%fused_computation.8 | loop fusion | flops 3932160 | bytes 6293504 | tf_op jit(solution)/shard_map/convert_element_type | solution.py:100
  74.9 4.7 %all-to-all-start.2 = ((bf16[8,4,8,3072]{3,2,1,0:T(8,128)(2,1)}), bf16[8,4,8,3072]{3,2,1,0:T(8,128)(2,1)S(1)}, u32[]{:S(2)}, u32[]{:S(2)}) async-start(bf16[8,4,8,3072]{3,2,1,0:T(8,128)(2,1)} %bitcast.40), calls=%async_computation.2 | async-start | bytes 3145728 | tf_op jit(solution)/shard_map/all_to_all | solution.py:101
  79.6 0.1 collective-permute-start.5
  79.7 1.9 %fusion.10 = (bf16[256,1024]{1,0:T(8,128)(2,1)S(1)}, bf16[256,1024]{1,0:T(8,128)(2,1)S(1)}) fusion(f32[256,1024]{1,0:T(8,128)} %copy-done.3, f32[256]{0:T(256)S(1)} %fusion.36, f32[256]{0:T(256)S(1)} %get-tuple-element.7, s32[1024]{0:T(1024)S(1)} %get-tuple-element.23, s32[256]{0:T(256)S(1)} %eq.13, s32[1024]{0:T(1024)S(1)} %get-tuple-element.22, ...), kind=kLoop, calls=%fused_computation.21 | loop fusion | flops 3145728 | bytes 3156992 | tf_op jit(solution)/shard_map/convert_element_type | solution.py:105
  81.7 0.5 collective-permute-start.6
  82.1 1.7 %collective-permute-done.6 = bf16[256,1024]{1,0:T(8,128)(2,1)S(1)} collective-permute-done((bf16[256,1024]{1,0:T(8,128)(2,1)S(1)}, bf16[256,1024]{1,0:T(8,128)(2,1)S(1)}, u32[]{:S(2)}, u32[]{:S(2)}) %collective-permute-start.6) | collective-permute-done | bytes 524320 | tf_op jit(solution)/shard_map/ppermute | solution.py:32
  83.9 0.0 collective-permute-done.5
  83.9 5.4 %convolution_convert_fusion.refs_1_ = bf16[3072,1024]{1,0:T(8,128)(2,1)} fusion(bf16[256,3072]{1,0:T(8,128)(2,1)S(1)} %collective-permute-done.5, bf16[256,3072]{1,0:T(8,128)(2,1)S(1)} %bitcast.44, bf16[256,1024]{1,0:T(8,128)(2,1)S(1)} %collective-permute-done.6, bf16[256,1024]{1,0:T(8,128)(2,1)S(1)} %get-tuple-element.13), kind=kOutput, calls=%fused_computation | convolution fusion | flops 3232759808 | bytes 10485760 | tf_op jit(solution)/shard_map/dot_general | solution.py:110
  89.2 10.0 %all-to-all-done.2 = bf16[8,4,8,3072]{3,2,1,0:T(8,128)(2,1)S(1)} async-done(((bf16[8,4,8,3072]{3,2,1,0:T(8,128)(2,1)}), bf16[8,4,8,3072]{3,2,1,0:T(8,128)(2,1)S(1)}, u32[]{:S(2)}, u32[]{:S(2)}) %all-to-all-start.2) | async-done | bytes 1572896 | tf_op jit(solution)/shard_map/all_to_all | solution.py:101
  99.2 1.0 convert_reduce_fusion.refs_0_
  100.2 5.8 %all-to-all-start.3 = ((f32[4,8,3072]{2,1,0:T(8,128)}), f32[4,8,3072]{2,1,0:T(8,128)S(1)}, u32[]{:S(2)}, u32[]{:S(2)}) async-start(f32[4,8,3072]{2,1,0:T(8,128)} %shard_map.60), calls=%async_computation.3 | async-start | bytes 786432 | tf_op jit(solution)/shard_map/all_to_all | solution.py:114
  105.9 0.0 collective-permute-start.4
  105.9 1.2 %collective-permute-done.4 = f32[1]{0:T(128)} collective-permute-done((f32[1]{0:T(128)}, f32[1]{0:T(128)}, u32[]{:S(2)}, u32[]{:S(2)}) %collective-permute-start.4) | collective-permute-done | bytes 36 | tf_op jit(solution)/shard_map/ppermute | solution.py:32
  108.4 10.9 %all-to-all-done.3 = f32[4,8,3072]{2,1,0:T(8,128)S(1)} async-done(((f32[4,8,3072]{2,1,0:T(8,128)}), f32[4,8,3072]{2,1,0:T(8,128)S(1)}, u32[]{:S(2)}, u32[]{:S(2)}) %all-to-all-start.3) | async-done | bytes 393248 | tf_op jit(solution)/shard_map/all_to_all | solution.py:114
  119.4 0.6 reduce_sum.89
  (23 shorter events, 0.1 us)
Async XLA Ops:
  0.6 14.2 %collective-permute-start.3 = (bf16[3072,1024]{1,0:T(8,128)(2,1)}, bf16[3072,1024]{1,0:T(8,128)(2,1)}, u32[]{:S(2)}, u32[]{:S(2)}) collective-permute-start(bf16[3072,1024]{1,0:T(8,128)(2,1)} %param.4), channel_id=1, source_target_pairs={{0,1},{1,0},{2,3},{3,2},{4,5},{5,4},{6,7},{7,6},{8,9},{9,8},{10,11... | collective-permute-start | bytes 18874376 | tf_op jit(solution)/shard_map/ppermute | solution.py:32
  0.7 12.3 %collective-permute-start = (bf16[8,3072]{1,0:T(8,128)(2,1)}, bf16[8,3072]{1,0:T(8,128)(2,1)S(1)}, u32[]{:S(2)}, u32[]{:S(2)}) collective-permute-start(bf16[8,3072]{1,0:T(8,128)(2,1)} %param.3), channel_id=1, source_target_pairs={{0,32},{16,48},{32,0},{48,16},{1,33},{17,49},{33,1},{49,17},{2,34}... | collective-permute-start | bytes 147464 | tf_op jit(solution)/shard_map/ppermute | solution.py:24
  8.0 6.4 %collective-permute-start.1 = (bf16[8,3072]{1,0:T(8,128)(2,1)}, bf16[8,3072]{1,0:T(8,128)(2,1)S(1)}, u32[]{:S(2)}, u32[]{:S(2)}) collective-permute-start(bf16[8,3072]{1,0:T(8,128)(2,1)} %param.3), channel_id=1, source_target_pairs={{0,16},{16,32},{32,48},{48,0},{1,17},{17,33},{33,49},{49,1},{2,18}... | collective-permute-start | bytes 147464 | tf_op jit(solution)/shard_map/ppermute | solution.py:24
  9.5 5.3 %collective-permute-start.2 = (bf16[8,3072]{1,0:T(8,128)(2,1)}, bf16[8,3072]{1,0:T(8,128)(2,1)S(1)}, u32[]{:S(2)}, u32[]{:S(2)}) collective-permute-start(bf16[8,3072]{1,0:T(8,128)(2,1)} %param.3), channel_id=1, source_target_pairs={{0,48},{16,0},{32,16},{48,32},{1,49},{17,1},{33,17},{49,33},{2,50}... | collective-permute-start | bytes 147464 | tf_op jit(solution)/shard_map/ppermute | solution.py:24
  14.8 6.7 %copy-start.6 = (s32[512]{0:T(512)S(1)}, s32[512]{0:T(512)}, u32[]{:S(2)}) copy-start(s32[512]{0:T(512)} %param.5) | copy-start | bytes 6148
  16.1 24.2 %all-to-all-start = ((bf16[8,4,8,3072]{3,2,1,0:T(8,128)(2,1)}), bf16[8,4,8,3072]{3,2,1,0:T(8,128)(2,1)S(1)}, u32[]{:S(2)}, u32[]{:S(2)}) async-start(bf16[8,4,8,3072]{3,2,1,0:T(8,128)(2,1)} %broadcast_in_dim.50), calls=%async_computation | async-start | bytes 3145728 | tf_op jit(solution)/shard_map/all_to_all | solution.py:16
  40.3 5.2 %copy-start.4 = (bf16[8,4,8,3072]{3,2,1,0:T(8,128)(2,1)}, bf16[8,4,8,3072]{3,2,1,0:T(8,128)(2,1)S(1)}, u32[]{:S(2)}) copy-start(bf16[8,4,8,3072]{3,2,1,0:T(8,128)(2,1)S(1)} %all-to-all-done) | copy-start | bytes 4718596
  45.6 15.0 %copy-start.3 = (f32[256,1024]{1,0:T(8,128)}, f32[256,1024]{1,0:T(8,128)S(1)}, u32[]{:S(2)}) copy-start(f32[256,1024]{1,0:T(8,128)S(1)} %get-tuple-element.19) | copy-start | bytes 3145732
  50.6 1.0 copy-start
  52.3 18.6 %all-to-all-start.1 = ((f32[32,3,256]{2,1,0:T(4,128)}), f32[32,3,256]{2,1,0:T(4,128)S(1)}, u32[]{:S(2)}, u32[]{:S(2)}) async-start(f32[32,3,256]{2,1,0:T(4,128)} %broadcast_in_dim.52), calls=%async_computation.1 | async-start | bytes 262144 | tf_op jit(solution)/shard_map/all_to_all | solution.py:16
  60.6 4.8 %copy-start.1 = (f32[256,1024]{1,0:T(8,128)S(1)}, f32[256,1024]{1,0:T(8,128)}, u32[]{:S(2)}) copy-start(f32[256,1024]{1,0:T(8,128)} %copy-done) | copy-start | bytes 3145732
  74.9 4.8 %copy-start.2 = (f32[256,1024]{1,0:T(8,128)S(1)}, f32[256,1024]{1,0:T(8,128)}, u32[]{:S(2)}) copy-start(f32[256,1024]{1,0:T(8,128)} %copy-done) | copy-start | bytes 3145732
  74.9 24.3 %all-to-all-start.2 = ((bf16[8,4,8,3072]{3,2,1,0:T(8,128)(2,1)}), bf16[8,4,8,3072]{3,2,1,0:T(8,128)(2,1)S(1)}, u32[]{:S(2)}, u32[]{:S(2)}) async-start(bf16[8,4,8,3072]{3,2,1,0:T(8,128)(2,1)} %bitcast.40), calls=%async_computation.2 | async-start | bytes 3145728 | tf_op jit(solution)/shard_map/all_to_all | solution.py:101
  79.6 4.3 %copy-start.5 = (bf16[8,4,8,3072]{3,2,1,0:T(8,128)(2,1)S(1)}, bf16[8,4,8,3072]{3,2,1,0:T(8,128)(2,1)}, u32[]{:S(2)}) copy-start(bf16[8,4,8,3072]{3,2,1,0:T(8,128)(2,1)} %copy-done.4) | copy-start | bytes 4718596
  79.6 4.2 %collective-permute-start.5 = (bf16[256,3072]{1,0:T(8,128)(2,1)}, bf16[256,3072]{1,0:T(8,128)(2,1)S(1)}, u32[]{:S(2)}, u32[]{:S(2)}) collective-permute-start(bf16[256,3072]{1,0:T(8,128)(2,1)} %bitcast.43), channel_id=1, source_target_pairs={{0,1},{1,0},{2,3},{3,2},{4,5},{5,4},{6,7},{7,6},{8,9},{9,8},{10,11... | collective-permute-start | bytes 4718600 | tf_op jit(solution)/shard_map/ppermute | solution.py:32
  81.7 2.2 %collective-permute-start.6 = (bf16[256,1024]{1,0:T(8,128)(2,1)S(1)}, bf16[256,1024]{1,0:T(8,128)(2,1)S(1)}, u32[]{:S(2)}, u32[]{:S(2)}) collective-permute-start(bf16[256,1024]{1,0:T(8,128)(2,1)S(1)} %get-tuple-element.14), channel_id=1, source_target_pairs={{0,1},{1,0},{2,3},{3,2},{4,5},{5,4},{6,7},{7,6},{8,9},{9,8},{10,11... | collective-permute-start | bytes 1572872 | tf_op jit(solution)/shard_map/ppermute | solution.py:32
  100.2 19.2 %all-to-all-start.3 = ((f32[4,8,3072]{2,1,0:T(8,128)}), f32[4,8,3072]{2,1,0:T(8,128)S(1)}, u32[]{:S(2)}, u32[]{:S(2)}) async-start(f32[4,8,3072]{2,1,0:T(8,128)} %shard_map.60), calls=%async_computation.3 | async-start | bytes 786432 | tf_op jit(solution)/shard_map/all_to_all | solution.py:114
  105.9 1.2 %collective-permute-start.4 = (f32[1]{0:T(128)}, f32[1]{0:T(128)}, u32[]{:S(2)}, u32[]{:S(2)}) collective-permute-start(f32[1]{0:T(128)} %bitcast.11), channel_id=1, source_target_pairs={{0,1},{1,0},{2,3},{3,2},{4,5},{5,4},{6,7},{7,6},{8,9},{9,8},{10,11... | collective-permute-start | bytes 20 | tf_op jit(solution)/shard_map/ppermute | solution.py:32

commit v2 on v1

--- a/solution.py
+++ b/solution.py
@@ -18,14 +18,32 @@
     )
 
 
+def shifts(n):
+    return sorted(range(1, n), key=lambda k: -min(k, n - k))
+
+
+def shifted(value, axis, by):
+    n = lax.axis_size(axis)
+    return lax.ppermute(value, axis, [(i, (i + by) % n) for i in range(n)])
+
+
 def from_each(value, axis):
     n, me = lax.axis_size(axis), lax.axis_index(axis)
-    shifts = sorted(range(1, n), key=lambda k: -min(k, n - k))
-    pieces = [(k, lax.ppermute(value, axis, [(i, (i + k) % n) for i in range(n)])) for k in shifts]
+    pieces = [(k, shifted(value, axis, k)) for k in shifts(n)]
     found = jnp.zeros((n, *value.shape), value.dtype)
     for k, piece in [(0, value)] + pieces:
         found = lax.dynamic_update_index_in_dim(found, piece, lax.rem(me - k + n, n), 0)
     return found
+
+
+def summed_at(value, axis):
+    n, me = lax.axis_size(axis), lax.axis_index(axis)
+
+    def entry(k):
+        return lax.dynamic_index_in_dim(value, lax.rem(me - k + n, n), 0, keepdims=False)
+
+    arrived = [shifted(entry(k), axis, -k) for k in shifts(n)]
+    return sum(arrived, entry(0))
 
 
 def swapped(value):
@@ -111,12 +129,12 @@
         both, own, (((0,), (0,)), ((), ())), preferred_element_type=jnp.float32
     ).astype(jnp.bfloat16)
 
-    summed = lax.all_to_all(after(summed, d_weight), "zh", 0, 0, tiled=True)
-    d_hidden = jnp.sum(summed, axis=0).astype(jnp.bfloat16)
+    part = jnp.sum(top + jnp.log(total) - picked).reshape(1, 1)
+    loss = (part + swapped(part)) / (2 * tokens)
 
-    part = jnp.sum(top + jnp.log(total) - picked).reshape(1)
-    loss = (part + swapped(part)) / (2 * tokens)
-    return (loss, d_hidden, d_weight)
+    summed = after(after(summed, d_weight), loss, pl.ANY)
+    d_hidden = summed_at(summed, "zh").astype(jnp.bfloat16)
+    return (loss.reshape(1), d_hidden, d_weight)
 
 
 def solution(mesh):

time: 122 us -> 118 us (0.967)
  waiting for transfers between devices: 34.5 us -> 28 us
  starting transfers between devices: 36.1 us -> 39.2 us
    all_to_all x1 -> x0, waiting for transfers between devices: 10.9 us -> none  [body(): summed = lax.all_to_all(after(summed, d_weight), 'zh', 0, 0, tiled=True)]
    ppermute x3 -> x6, starting transfers between devices: 11.4 us -> 20.1 us  [shifted(): return lax.ppermute(value, axis, [(i, (i + by) % n) for i in range(n)])]
    ppermute x3 -> x6, waiting for transfers between devices: 1.78 us -> 8.91 us  [shifted(): return lax.ppermute(value, axis, [(i, (i + by) % n) for i in range(n)])]
    all_to_all x1 -> x0, starting transfers between devices: 5.77 us -> none  [body(): summed = lax.all_to_all(after(summed, d_weight), 'zh', 0, 0, tiled=True)]
    all_to_all x1, waiting for transfers between devices: 9.97 us -> 8.5 us  [body(): summed = lax.all_to_all(partial, NEAR, 0, 0, tiled=True)]
    ppermute x4, waiting for transfers between devices: 2.95 us -> 1.67 us  [swapped(): return lax.ppermute(value, 'core', SWAP)]
  transfers between devices with their start and end apart: 11 -> 13, of which waited for: 8 -> 8; matrix products, arithmetic and copies ran while one was open for 23% -> 24% of each run, Pallas kernels for 0% -> 0%
where the time goes in v2:
time: 118 us; the launch traced here: 117 us
  starting transfers between devices  39.2 us (33%)
  matrix products  35.6 us (30%)
  waiting for transfers between devices  28 us (24%)
  other arithmetic  7.5 us (6%)
  local copies, waits for them, and re-layouts  3.44 us (3%)
  between operations  3.4 us (3%)
    ppermute x6, starting transfers between devices, shifted(): return lax.ppermute(value, axis, [(i, (i + by) % n) for i in range(n)])  20.1 us
    dot_general x4, matrix products, back(): lax.dot_general(grads, columns, (((1,), (1,)), ((), ())), preferred_eleme...  20 us
    all_to_all x2, starting transfers between devices, to_each(): lax.all_to_all(jnp.broadcast_to(value[None], (devices, *value.shape)), ax...  13.6 us
    dot_general x2, matrix products, body(): jnp.dot(mine, w, preferred_element_type=jnp.float32)  10.3 us
    ppermute x6, waiting for transfers between devices, shifted(): return lax.ppermute(value, axis, [(i, (i + by) % n) for i in range(n)])  8.91 us
    all_to_all x2, waiting for transfers between devices, to_each(): lax.all_to_all(jnp.broadcast_to(value[None], (devices, *value.shape)), ax...  8.88 us
    all_to_all x1, waiting for transfers between devices, body(): summed = lax.all_to_all(partial, NEAR, 0, 0, tiled=True)  8.5 us
    dot_general x1, matrix products, body(): lax.dot_general(both, own, (((0,), (0,)), ((), ())), preferred_element_ty...  5.39 us
  transfers between devices with their start and end apart: 13, of which 8 were waited for; matrix products, arithmetic and copies ran while one was open for 24% of the time, Pallas kernels for 0%

profile of v2, /device:TPU:4, one launch (start us, length us, event | category | flops | bytes accessed | tf_op | source)
XLA Modules:
  0.0 117.1 jit_solution(14272127002780670622)
XLA Ops:
  0.6 0.1 collective-permute-start.3
  0.7 7.3 %collective-permute-start = (bf16[8,3072]{1,0:T(8,128)(2,1)}, bf16[8,3072]{1,0:T(8,128)(2,1)S(1)}, u32[]{:S(2)}, u32[]{:S(2)}) collective-permute-start(bf16[8,3072]{1,0:T(8,128)(2,1)} %param.3), channel_id=1, source_target_pairs={{0,32},{16,48},{32,0},{48,16},{1,33},{17,49},{33,1},{49,17},{2,34}... | collective-permute-start | bytes 147464 | tf_op jit(solution)/shard_map/ppermute | solution.py:27
  8.0 1.5 %collective-permute-start.1 = (bf16[8,3072]{1,0:T(8,128)(2,1)}, bf16[8,3072]{1,0:T(8,128)(2,1)S(1)}, u32[]{:S(2)}, u32[]{:S(2)}) collective-permute-start(bf16[8,3072]{1,0:T(8,128)(2,1)} %param.3), channel_id=1, source_target_pairs={{0,16},{16,32},{32,48},{48,0},{1,17},{17,33},{33,49},{49,1},{2,18}... | collective-permute-start | bytes 147464 | tf_op jit(solution)/shard_map/ppermute | solution.py:27
  9.5 2.7 %collective-permute-start.2 = (bf16[8,3072]{1,0:T(8,128)(2,1)}, bf16[8,3072]{1,0:T(8,128)(2,1)S(1)}, u32[]{:S(2)}, u32[]{:S(2)}) collective-permute-start(bf16[8,3072]{1,0:T(8,128)(2,1)} %param.3), channel_id=1, source_target_pairs={{0,48},{16,0},{32,16},{48,32},{1,49},{17,1},{33,17},{49,33},{2,50}... | collective-permute-start | bytes 147464 | tf_op jit(solution)/shard_map/ppermute | solution.py:27
  12.2 0.8 bitcast_dynamic-update-slice_fusion.3
  13.0 0.0 collective-permute-done
  13.0 1.4 %collective-permute-done.1 = bf16[8,3072]{1,0:T(8,128)(2,1)S(1)} collective-permute-done((bf16[8,3072]{1,0:T(8,128)(2,1)}, bf16[8,3072]{1,0:T(8,128)(2,1)S(1)}, u32[]{:S(2)}, u32[]{:S(2)}) %collective-permute-start.1) | collective-permute-done | bytes 49184 | tf_op jit(solution)/shard_map/ppermute | solution.py:27
  14.4 0.4 collective-permute-done.2
  14.8 0.0 collective-permute-done.3.refs_1_
  14.8 0.0 copy-start.6
  14.8 1.3 %broadcast_in_dim.50 = bf16[8,4,8,3072]{3,2,1,0:T(8,128)(2,1)} broadcast(bf16[4,8,3072]{2,1,0:T(8,128)(2,1)S(1)} %shard_map.58), dimensions={1,2,3} | broadcast | bytes 1769472 | tf_op jit(solution)/shard_map/broadcast_in_dim | solution.py:17
  16.1 5.4 %all-to-all-start = ((bf16[8,4,8,3072]{3,2,1,0:T(8,128)(2,1)}), bf16[8,4,8,3072]{3,2,1,0:T(8,128)(2,1)S(1)}, u32[]{:S(2)}, u32[]{:S(2)}) async-start(bf16[8,4,8,3072]{3,2,1,0:T(8,128)(2,1)} %broadcast_in_dim.50), calls=%async_computation | async-start | bytes 3145728 | tf_op jit(solution)/shard_map/all_to_all | solution.py:16
  21.5 0.1 reshape.103
  21.7 0.1 eq.13
  21.8 4.6 %fusion.5 = f32[256,3072]{1,0:T(8,128)S(1)} fusion(bf16[3072,1024]{1,0:T(8,128)(2,1)} %param.4, s32[1024]{0:T(1024)S(1)} %get-tuple-element.26, s32[256]{0:T(256)S(1)} %eq.13), kind=kOutput, calls=%fused_computation.14 | convolution fusion | flops 1610874880 | bytes 9442304 | tf_op jit(solution)/shard_map/dot_general | solution.py:72
  26.4 5.8 %fusion = bf16[256,3072]{1,0:T(8,128)(2,1)} fusion(f32[256,3072]{1,0:T(8,128)S(1)} %fusion.5, bf16[3072,1024]{1,0:T(8,128)(2,1)} %collective-permute-done.3.refs_1_, s32[1024]{0:T(1024)S(1)} %get-tuple-element.25, s32[256]{0:T(256)S(1)} %eq.13), kind=kOutput, calls=%fused_computation.3 | convolution fusion | flops 1612447744 | bytes 11015168 | tf_op jit(solution)/shard_map/dot_general | solution.py:72
  32.2 8.1 %all-to-all-done = bf16[8,4,8,3072]{3,2,1,0:T(8,128)(2,1)S(1)} async-done(((bf16[8,4,8,3072]{3,2,1,0:T(8,128)(2,1)}), bf16[8,4,8,3072]{3,2,1,0:T(8,128)(2,1)S(1)}, u32[]{:S(2)}, u32[]{:S(2)}) %all-to-all-start) | async-done | bytes 1572896 | tf_op jit(solution)/shard_map/all_to_all | solution.py:16
  40.3 5.2 %fusion.44 = (f32[256]{0:T(256)S(1)}, f32[256,1024]{1,0:T(8,128)S(1)}) fusion(bf16[256,3072]{1,0:T(8,128)(2,1)S(1)} %bitcast.56, bf16[3072,1024]{1,0:T(8,128)(2,1)} %param.4), kind=kOutput, calls=%fused_computation.74 | convolution fusion | flops 1610874624 | bytes 8913920 | tf_op jit(solution)/shard_map/dot_general | solution.py:99
  45.6 5.0 %fusion.45 = (f32[256]{0:T(256)S(1)}, f32[256,1024]{1,0:T(8,128)S(1)}) fusion(bf16[256,3072]{1,0:T(8,128)(2,1)S(1)} %bitcast.57, bf16[3072,1024]{1,0:T(8,128)(2,1)} %collective-permute-done.3.refs_1_), kind=kOutput, calls=%fused_computation.75 | convolution fusion | flops 1610874624 | bytes 8913920 | tf_op jit(solution)/shard_map/dot_general | solution.py:99
  50.6 0.7 exponential_reduce_fusion.1
  51.3 0.3 copy-done
  51.7 0.7 broadcast_in_dim.52
  52.3 8.2 %all-to-all-start.1 = ((f32[32,3,256]{2,1,0:T(4,128)}), f32[32,3,256]{2,1,0:T(4,128)S(1)}, u32[]{:S(2)}, u32[]{:S(2)}) async-start(f32[32,3,256]{2,1,0:T(4,128)} %broadcast_in_dim.52), calls=%async_computation.1 | async-start | bytes 262144 | tf_op jit(solution)/shard_map/all_to_all | solution.py:16
  60.6 4.8 %fusion.19 = f32[256,3072]{1,0:T(8,128)S(1)} fusion(bf16[3072,1024]{1,0:T(8,128)(2,1)} %param.4, f32[256,1024]{1,0:T(8,128)S(1)} %get-tuple-element.22, f32[256]{0:T(256)S(1)} %bitcast.61, s32[1024]{0:T(1024)S(1)} %get-tuple-element.26, s32[256]{0:T(256)S(1)} %eq.13), kind=kOutput, calls=%fused_computation.31 | convolution fusion | flops 1611661312 | bytes 10491904 | tf_op jit(solution)/shard_map/dot_general | solution.py:72
  65.4 4.8 %convolution_add_fusion = f32[256,3072]{1,0:T(8,128)S(1)} fusion(f32[256,3072]{1,0:T(8,128)S(1)} %fusion.19, bf16[3072,1024]{1,0:T(8,128)(2,1)} %collective-permute-done.3.refs_1_, f32[256,1024]{1,0:T(8,128)S(1)} %copy-done.1, f32[256]{0:T(256)S(1)} %bitcast.62, s32[1024]{0:T(1024)S(1)} %get-tuple-element.25, s32[256]{0:T(256)S(1)} %eq.13), kind=kOutput, calls=%fused_computation.1 | convolution fusion | flops 1612447744 | bytes 13637632 | tf_op jit(solution)/shard_map/dot_general | solution.py:72
  70.2 0.8 all-to-all-done.1
  70.9 0.1 slice_reduce_fusion.1
  71.1 0.6 fusion.40
  71.7 3.3 %add_convert_fusion = bf16[256,3072]{1,0:T(8,128)(2,1)} fusion(bf16[256,3072]{1,0:T(8,128)(2,1)} %fusion, f32[256,3072]{1,0:T(8,128)S(1)} %convolution_add_fusion, f32[256]{0:T(256)S(1)} %get-tuple-element.18, f32[256]{0:T(256)S(1)} %get-tuple-element.20), kind=kLoop, calls=%fused_computation.8 | loop fusion | flops 3932160 | bytes 6293504 | tf_op jit(solution)/shard_map/convert_element_type | solution.py:118
  74.9 4.7 %all-to-all-start.2 = ((bf16[8,4,8,3072]{3,2,1,0:T(8,128)(2,1)}), bf16[8,4,8,3072]{3,2,1,0:T(8,128)(2,1)S(1)}, u32[]{:S(2)}, u32[]{:S(2)}) async-start(bf16[8,4,8,3072]{3,2,1,0:T(8,128)(2,1)} %bitcast.55), calls=%async_computation.2 | async-start | bytes 3145728 | tf_op jit(solution)/shard_map/all_to_all | solution.py:119
  79.6 0.1 collective-permute-start.5
  79.7 0.0 copy-done.2
  79.7 1.9 %fusion.10 = (bf16[256,1024]{1,0:T(8,128)(2,1)S(1)}, bf16[256,1024]{1,0:T(8,128)(2,1)S(1)}) fusion(f32[256,1024]{1,0:T(8,128)} %copy-done.3, f32[256]{0:T(256)S(1)} %fusion.39, f32[256]{0:T(256)S(1)} %get-tuple-element.7, s32[1024]{0:T(1024)S(1)} %get-tuple-element.26, s32[256]{0:T(256)S(1)} %eq.13, s32[1024]{0:T(1024)S(1)} %get-tuple-element.25, ...), kind=kLoop, calls=%fused_computation.21 | loop fusion | flops 3145728 | bytes 3156992 | tf_op jit(solution)/shard_map/convert_element_type | solution.py:123
  81.7 0.5 collective-permute-start.6
  82.1 0.1 collective-permute-start.4
  82.3 1.7 %collective-permute-done.4 = f32[1,1]{1,0:T(1,128)} collective-permute-done((f32[1,1]{1,0:T(1,128)}, f32[1,1]{1,0:T(1,128)}, u32[]{:S(2)}, u32[]{:S(2)}) %collective-permute-start.4) | collective-permute-done | bytes 36 | tf_op jit(solution)/shard_map/ppermute | solution.py:50
  85.3 0.0 collective-permute-done.6
  85.3 0.0 collective-permute-done.5
  85.3 5.4 %convolution_convert_fusion.refs_1_ = bf16[3072,1024]{1,0:T(8,128)(2,1)} fusion(bf16[256,3072]{1,0:T(8,128)(2,1)S(1)} %collective-permute-done.5, bf16[256,3072]{1,0:T(8,128)(2,1)S(1)} %bitcast.59, bf16[256,1024]{1,0:T(8,128)(2,1)S(1)} %collective-permute-done.6, bf16[256,1024]{1,0:T(8,128)(2,1)S(1)} %get-tuple-element.16), kind=kOutput, calls=%fused_computation | convolution fusion | flops 3232759808 | bytes 10485760 | tf_op jit(solution)/shard_map/dot_general | solution.py:128
  90.7 8.5 %all-to-all-done.2 = bf16[8,4,8,3072]{3,2,1,0:T(8,128)(2,1)S(1)} async-done(((bf16[8,4,8,3072]{3,2,1,0:T(8,128)(2,1)}), bf16[8,4,8,3072]{3,2,1,0:T(8,128)(2,1)S(1)}, u32[]{:S(2)}, u32[]{:S(2)}) %all-to-all-start.2) | async-done | bytes 1572896 | tf_op jit(solution)/shard_map/all_to_all | solution.py:119
  99.2 0.2 convert_reduce_fusion.refs_0_
  99.5 2.4 %collective-permute-start.9 = (f32[8,3072]{1,0:T(8,128)S(1)}, f32[8,3072]{1,0:T(8,128)S(1)}, u32[]{:S(2)}, u32[]{:S(2)}) collective-permute-start(f32[8,3072]{1,0:T(8,128)S(1)} %get-tuple-element.12), channel_id=1, source_target_pairs={{0,16},{16,32},{32,48},{48,0},{1,17},{17,33},{33,49},{49,1},{2,18}... | collective-permute-start | bytes 294920 | tf_op jit(solution)/shard_map/ppermute | solution.py:27
  101.9 1.8 %collective-permute-start.8 = (f32[8,3072]{1,0:T(8,128)S(1)}, f32[8,3072]{1,0:T(8,128)S(1)}, u32[]{:S(2)}, u32[]{:S(2)}) collective-permute-start(f32[8,3072]{1,0:T(8,128)S(1)} %get-tuple-element.13), channel_id=1, source_target_pairs={{0,48},{16,0},{32,16},{48,32},{1,49},{17,1},{33,17},{49,33},{2,50}... | collective-permute-start | bytes 294920 | tf_op jit(solution)/shard_map/ppermute | solution.py:27
  103.7 4.5 %collective-permute-start.7 = (f32[8,3072]{1,0:T(8,128)S(1)}, f32[8,3072]{1,0:T(8,128)S(1)}, u32[]{:S(2)}, u32[]{:S(2)}) collective-permute-start(f32[8,3072]{1,0:T(8,128)S(1)} %get-tuple-element.11), channel_id=1, source_target_pairs={{0,32},{16,48},{32,0},{48,16},{1,33},{17,49},{33,1},{49,17},{2,34}... | collective-permute-start | bytes 294920 | tf_op jit(solution)/shard_map/ppermute | solution.py:27
  108.2 0.0 collective-permute-done.9
  108.2 0.8 collective-permute-done.8
  109.0 6.3 %collective-permute-done.7 = f32[8,3072]{1,0:T(8,128)S(1)} collective-permute-done((f32[8,3072]{1,0:T(8,128)S(1)}, f32[8,3072]{1,0:T(8,128)S(1)}, u32[]{:S(2)}, u32[]{:S(2)}) %collective-permute-start.7) | collective-permute-done | bytes 98336 | tf_op jit(solution)/shard_map/ppermute | solution.py:27
  115.3 0.6 fusion.35
  (29 shorter events, 0.2 us)
Async XLA Ops:
  0.6 14.2 %collective-permute-start.3 = (bf16[3072,1024]{1,0:T(8,128)(2,1)}, bf16[3072,1024]{1,0:T(8,128)(2,1)}, u32[]{:S(2)}, u32[]{:S(2)}) collective-permute-start(bf16[3072,1024]{1,0:T(8,128)(2,1)} %param.4), channel_id=1, source_target_pairs={{0,1},{1,0},{2,3},{3,2},{4,5},{5,4},{6,7},{7,6},{8,9},{9,8},{10,11... | collective-permute-start | bytes 18874376 | tf_op jit(solution)/shard_map/ppermute | solution.py:50
  0.7 12.3 %collective-permute-start = (bf16[8,3072]{1,0:T(8,128)(2,1)}, bf16[8,3072]{1,0:T(8,128)(2,1)S(1)}, u32[]{:S(2)}, u32[]{:S(2)}) collective-permute-start(bf16[8,3072]{1,0:T(8,128)(2,1)} %param.3), channel_id=1, source_target_pairs={{0,32},{16,48},{32,0},{48,16},{1,33},{17,49},{33,1},{49,17},{2,34}... | collective-permute-start | bytes 147464 | tf_op jit(solution)/shard_map/ppermute | solution.py:27
  8.0 6.4 %collective-permute-start.1 = (bf16[8,3072]{1,0:T(8,128)(2,1)}, bf16[8,3072]{1,0:T(8,128)(2,1)S(1)}, u32[]{:S(2)}, u32[]{:S(2)}) collective-permute-start(bf16[8,3072]{1,0:T(8,128)(2,1)} %param.3), channel_id=1, source_target_pairs={{0,16},{16,32},{32,48},{48,0},{1,17},{17,33},{33,49},{49,1},{2,18}... | collective-permute-start | bytes 147464 | tf_op jit(solution)/shard_map/ppermute | solution.py:27
  9.5 5.3 %collective-permute-start.2 = (bf16[8,3072]{1,0:T(8,128)(2,1)}, bf16[8,3072]{1,0:T(8,128)(2,1)S(1)}, u32[]{:S(2)}, u32[]{:S(2)}) collective-permute-start(bf16[8,3072]{1,0:T(8,128)(2,1)} %param.3), channel_id=1, source_target_pairs={{0,48},{16,0},{32,16},{48,32},{1,49},{17,1},{33,17},{49,33},{2,50}... | collective-permute-start | bytes 147464 | tf_op jit(solution)/shard_map/ppermute | solution.py:27
  14.8 6.7 %copy-start.6 = (s32[512]{0:T(512)S(1)}, s32[512]{0:T(512)}, u32[]{:S(2)}) copy-start(s32[512]{0:T(512)} %param.5) | copy-start | bytes 6148
  16.1 24.2 %all-to-all-start = ((bf16[8,4,8,3072]{3,2,1,0:T(8,128)(2,1)}), bf16[8,4,8,3072]{3,2,1,0:T(8,128)(2,1)S(1)}, u32[]{:S(2)}, u32[]{:S(2)}) async-start(bf16[8,4,8,3072]{3,2,1,0:T(8,128)(2,1)} %broadcast_in_dim.50), calls=%async_computation | async-start | bytes 3145728 | tf_op jit(solution)/shard_map/all_to_all | solution.py:16
  40.3 5.2 %copy-start.4 = (bf16[8,4,8,3072]{3,2,1,0:T(8,128)(2,1)}, bf16[8,4,8,3072]{3,2,1,0:T(8,128)(2,1)S(1)}, u32[]{:S(2)}) copy-start(bf16[8,4,8,3072]{3,2,1,0:T(8,128)(2,1)S(1)} %all-to-all-done) | copy-start | bytes 4718596
  45.6 15.0 %copy-start.3 = (f32[256,1024]{1,0:T(8,128)}, f32[256,1024]{1,0:T(8,128)S(1)}, u32[]{:S(2)}) copy-start(f32[256,1024]{1,0:T(8,128)S(1)} %get-tuple-element.22) | copy-start | bytes 3145732
  50.6 1.0 copy-start
  52.3 18.6 %all-to-all-start.1 = ((f32[32,3,256]{2,1,0:T(4,128)}), f32[32,3,256]{2,1,0:T(4,128)S(1)}, u32[]{:S(2)}, u32[]{:S(2)}) async-start(f32[32,3,256]{2,1,0:T(4,128)} %broadcast_in_dim.52), calls=%async_computation.1 | async-start | bytes 262144 | tf_op jit(solution)/shard_map/all_to_all | solution.py:16
  60.6 4.8 %copy-start.1 = (f32[256,1024]{1,0:T(8,128)S(1)}, f32[256,1024]{1,0:T(8,128)}, u32[]{:S(2)}) copy-start(f32[256,1024]{1,0:T(8,128)} %copy-done) | copy-start | bytes 3145732
  74.9 4.8 %copy-start.2 = (f32[256,1024]{1,0:T(8,128)S(1)}, f32[256,1024]{1,0:T(8,128)}, u32[]{:S(2)}) copy-start(f32[256,1024]{1,0:T(8,128)} %copy-done) | copy-start | bytes 3145732
  74.9 24.3 %all-to-all-start.2 = ((bf16[8,4,8,3072]{3,2,1,0:T(8,128)(2,1)}), bf16[8,4,8,3072]{3,2,1,0:T(8,128)(2,1)S(1)}, u32[]{:S(2)}, u32[]{:S(2)}) async-start(bf16[8,4,8,3072]{3,2,1,0:T(8,128)(2,1)} %bitcast.55), calls=%async_computation.2 | async-start | bytes 3145728 | tf_op jit(solution)/shard_map/all_to_all | solution.py:119
  79.6 5.7 %copy-start.5 = (bf16[8,4,8,3072]{3,2,1,0:T(8,128)(2,1)S(1)}, bf16[8,4,8,3072]{3,2,1,0:T(8,128)(2,1)}, u32[]{:S(2)}) copy-start(bf16[8,4,8,3072]{3,2,1,0:T(8,128)(2,1)} %copy-done.4) | copy-start | bytes 4718596
  79.6 5.7 %collective-permute-start.5 = (bf16[256,3072]{1,0:T(8,128)(2,1)}, bf16[256,3072]{1,0:T(8,128)(2,1)S(1)}, u32[]{:S(2)}, u32[]{:S(2)}) collective-permute-start(bf16[256,3072]{1,0:T(8,128)(2,1)} %bitcast.58), channel_id=1, source_target_pairs={{0,1},{1,0},{2,3},{3,2},{4,5},{5,4},{6,7},{7,6},{8,9},{9,8},{10,11... | collective-permute-start | bytes 4718600 | tf_op jit(solution)/shard_map/ppermute | solution.py:50
  81.7 3.6 %collective-permute-start.6 = (bf16[256,1024]{1,0:T(8,128)(2,1)S(1)}, bf16[256,1024]{1,0:T(8,128)(2,1)S(1)}, u32[]{:S(2)}, u32[]{:S(2)}) collective-permute-start(bf16[256,1024]{1,0:T(8,128)(2,1)S(1)} %get-tuple-element.17), channel_id=1, source_target_pairs={{0,1},{1,0},{2,3},{3,2},{4,5},{5,4},{6,7},{7,6},{8,9},{9,8},{10,11... | collective-permute-start | bytes 1572872 | tf_op jit(solution)/shard_map/ppermute | solution.py:50
  82.1 1.8 %collective-permute-start.4 = (f32[1,1]{1,0:T(1,128)}, f32[1,1]{1,0:T(1,128)}, u32[]{:S(2)}, u32[]{:S(2)}) collective-permute-start(f32[1,1]{1,0:T(1,128)} %bitcast.11), channel_id=1, source_target_pairs={{0,1},{1,0},{2,3},{3,2},{4,5},{5,4},{6,7},{7,6},{8,9},{9,8},{10,11... | collective-permute-start | bytes 20 | tf_op jit(solution)/shard_map/ppermute | solution.py:50
  99.5 8.7 %collective-permute-start.9 = (f32[8,3072]{1,0:T(8,128)S(1)}, f32[8,3072]{1,0:T(8,128)S(1)}, u32[]{:S(2)}, u32[]{:S(2)}) collective-permute-start(f32[8,3072]{1,0:T(8,128)S(1)} %get-tuple-element.12), channel_id=1, source_target_pairs={{0,16},{16,32},{32,48},{48,0},{1,17},{17,33},{33,49},{49,1},{2,18}... | collective-permute-start | bytes 294920 | tf_op jit(solution)/shard_map/ppermute | solution.py:27
  101.9 7.1 %collective-permute-start.8 = (f32[8,3072]{1,0:T(8,128)S(1)}, f32[8,3072]{1,0:T(8,128)S(1)}, u32[]{:S(2)}, u32[]{:S(2)}) collective-permute-start(f32[8,3072]{1,0:T(8,128)S(1)} %get-tuple-element.13), channel_id=1, source_target_pairs={{0,48},{16,0},{32,16},{48,32},{1,49},{17,1},{33,17},{49,33},{2,50}... | collective-permute-start | bytes 294920 | tf_op jit(solution)/shard_map/ppermute | solution.py:27
  103.7 11.6 %collective-permute-start.7 = (f32[8,3072]{1,0:T(8,128)S(1)}, f32[8,3072]{1,0:T(8,128)S(1)}, u32[]{:S(2)}, u32[]{:S(2)}) collective-permute-start(f32[8,3072]{1,0:T(8,128)S(1)} %get-tuple-element.11), channel_id=1, source_target_pairs={{0,32},{16,48},{32,0},{48,16},{1,33},{17,49},{33,1},{49,17},{2,34}... | collective-permute-start | bytes 294920 | tf_op jit(solution)/shard_map/ppermute | solution.py:27

commit v3 on v2

--- a/solution.py
+++ b/solution.py
@@ -74,6 +74,49 @@
     )
 
 
+def back_kernel(first_g, second_g, first_ref, second_ref, out_ref, first_held, second_held, sems):
+    tiles, tile, _ = first_held.shape
+    dims = (((1,), (1,)), ((), ()))
+
+    def copies(k):
+        rows = pl.ds(k * tile, tile)
+        return (
+            pltpu.make_async_copy(first_ref.at[rows], first_held.at[k], sems.at[0, k]),
+            pltpu.make_async_copy(second_ref.at[rows], second_held.at[k], sems.at[1, k]),
+        )
+
+    for k in range(tiles):
+        for copy in copies(k):
+            copy.start()
+    for k in range(tiles):
+        for copy in copies(k):
+            copy.wait()
+        out_ref[:, pl.ds(k * tile, tile)] = lax.dot_general(
+            first_g[...], first_held[k], dims, preferred_element_type=jnp.float32
+        ) + lax.dot_general(
+            second_g[...], second_held[k], dims, preferred_element_type=jnp.float32
+        )
+
+
+def back_both(grads, weights, tiles=3):
+    rows = grads[0].shape[0]
+    depth, width = weights[0].shape
+    held = pltpu.VMEM((tiles, depth // tiles, width), weights[0].dtype)
+    return pl.pallas_call(
+        back_kernel,
+        in_specs=[pl.BlockSpec(memory_space=m) for m in [pltpu.VMEM] * 2 + [pltpu.HBM] * 2],
+        out_specs=pl.BlockSpec(memory_space=pltpu.VMEM),
+        out_shape=jax.ShapeDtypeStruct((rows, depth), jnp.float32),
+        scratch_shapes=[held, held, pltpu.SemaphoreType.DMA((2, tiles))],
+        compiler_params=pltpu.CompilerParams(vmem_limit_bytes=24 * 1024 * 1024),
+        cost_estimate=pl.CostEstimate(
+            flops=4 * rows * depth * width,
+            bytes_accessed=4 * depth * width,
+            transcendentals=0,
+        ),
+    )(*grads, *(pltpu.with_memory_space_constraint(w, pltpu.HBM) for w in weights))
+
+
 def body(hidden, weight, targets):
     rows, depth = hidden.shape
     width = weight.shape[1]
@@ -107,7 +150,8 @@
     local_top = after(packed, packed[1:2], pl.ANY)[0]
     expo = [jnp.exp(x - local_top[:, None]) for x in logits]
     rest = [jnp.where(h, 0.0, e).astype(jnp.bfloat16) for h, e in zip(hits, expo)]
-    others = lax.optimization_barrier(back(rest[0], weights[0]) + back(rest[1], weights[1]))
+    others = back_both(rest, weights)
+    stats = after(stats, others, pl.ANY)
 
     top = jnp.max(stats[:, 0], axis=0)
     total = jnp.sum(stats[:, 1] * jnp.exp(stats[:, 0] - top[None]), axis=0)

time: 118 us -> 117 us (level)
  matrix products: 35.6 us -> 26.1 us
  Pallas kernels: 0.01 us -> 6.13 us
  waiting for transfers between devices: 28 us -> 33 us
  starting transfers between devices: 39.2 us -> 34.9 us
  local copies, waits for them, and re-layouts: 3.44 us -> 4.93 us
    dot_general x4 -> x2, matrix products: 20 us -> 10.4 us  [back(): lax.dot_general(grads, columns, (((1,), (1,)), ((), ())), preferred_eleme...]
    pallas_call x0 -> x1, Pallas kernels: none -> 6.12 us  [back_both(): pl.pallas_call(back_kernel, in_specs=[pl.BlockSpec(memory_space=m) for m...]
    all_to_all x2, waiting for transfers between devices: 8.88 us -> 13.2 us  [to_each(): lax.all_to_all(jnp.broadcast_to(value[None], (devices, *value.shape)), ax...]
    ppermute x6, starting transfers between devices: 20.1 us -> 17.2 us  [shifted(): return lax.ppermute(value, axis, [(i, (i + by) % n) for i in range(n)])]
    unnamed x14 -> x18, local copies, waits for them, and re-layouts: 0.35 us -> 1.84 us
    reduce_sum x1, other arithmetic: 0.22 us -> 1.67 us  [body(): summed = jnp.sum(summed.astype(jnp.float32), axis=0)]
    convert_element_type x1, other arithmetic: 3.25 us -> 1.85 us  [body(): partial = partial.astype(jnp.bfloat16).reshape(near, far, rows, depth)]
    convert_element_type x1, other arithmetic: 1.94 us -> 0.63 us  [body(): (jnp.exp(x - top[:, None]) / total[:, None] - h.astype(jnp.float32)).asty...]
  transfers between devices with their start and end apart: 13 -> 13, of which waited for: 8 -> 9; matrix products, arithmetic and copies ran while one was open for 24% -> 16% of each run, Pallas kernels for 0% -> 5%
where the time goes in v3:
time: 117 us; the launch traced here: 115 us
  starting transfers between devices  34.9 us (30%)
  waiting for transfers between devices  33 us (28%)
  matrix products  26.1 us (22%)
  other arithmetic  6.76 us (6%)
  Pallas kernels  6.13 us (5%)
  local copies, waits for them, and re-layouts  4.93 us (4%)
  between operations  3.39 us (3%)
    ppermute x6, starting transfers between devices, shifted(): return lax.ppermute(value, axis, [(i, (i + by) % n) for i in range(n)])  17.2 us
    all_to_all x2, waiting for transfers between devices, to_each(): lax.all_to_all(jnp.broadcast_to(value[None], (devices, *value.shape)), ax...  13.2 us
    all_to_all x2, starting transfers between devices, to_each(): lax.all_to_all(jnp.broadcast_to(value[None], (devices, *value.shape)), ax...  12.4 us
    dot_general x2, matrix products, back(): lax.dot_general(grads, columns, (((1,), (1,)), ((), ())), preferred_eleme...  10.4 us
    dot_general x2, matrix products, body(): jnp.dot(mine, w, preferred_element_type=jnp.float32)  10.3 us
    ppermute x6, waiting for transfers between devices, shifted(): return lax.ppermute(value, axis, [(i, (i + by) % n) for i in range(n)])  9.01 us
    all_to_all x1, waiting for transfers between devices, body(): summed = lax.all_to_all(partial, NEAR, 0, 0, tiled=True)  8.72 us
    pallas_call x1, Pallas kernels, back_both(): pl.pallas_call(back_kernel, in_specs=[pl.BlockSpec(memory_space=m) for m...  6.12 us
  transfers between devices with their start and end apart: 13, of which 9 were waited for; matrix products, arithmetic and copies ran while one was open for 16% of the time, Pallas kernels for 5%

profile of v3, /device:TPU:4, one launch (start us, length us, event | category | flops | bytes accessed | tf_op | source)
XLA Modules:
  0.0 115.3 jit_solution(2599041916546374768)
XLA Ops:
  0.6 0.1 collective-permute-start.3
  0.7 7.3 %collective-permute-start = (bf16[8,3072]{1,0:T(8,128)(2,1)}, bf16[8,3072]{1,0:T(8,128)(2,1)S(1)}, u32[]{:S(2)}, u32[]{:S(2)}) collective-permute-start(bf16[8,3072]{1,0:T(8,128)(2,1)} %param.3), channel_id=1, source_target_pairs={{0,32},{16,48},{32,0},{48,16},{1,33},{17,49},{33,1},{49,17},{2,34}... | collective-permute-start | bytes 147464 | tf_op jit(solution)/shard_map/ppermute | solution.py:27
  8.0 0.0 collective-permute-start.2
  8.0 2.9 %collective-permute-start.1 = (bf16[8,3072]{1,0:T(8,128)(2,1)}, bf16[8,3072]{1,0:T(8,128)(2,1)S(1)}, u32[]{:S(2)}, u32[]{:S(2)}) collective-permute-start(bf16[8,3072]{1,0:T(8,128)(2,1)} %param.3), channel_id=1, source_target_pairs={{0,16},{16,32},{32,48},{48,0},{1,17},{17,33},{33,49},{49,1},{2,18}... | collective-permute-start | bytes 147464 | tf_op jit(solution)/shard_map/ppermute | solution.py:27
  11.0 0.8 bitcast_dynamic-update-slice_fusion.3
  11.8 0.0 collective-permute-done
  11.8 2.6 %collective-permute-done.1 = bf16[8,3072]{1,0:T(8,128)(2,1)S(1)} collective-permute-done((bf16[8,3072]{1,0:T(8,128)(2,1)}, bf16[8,3072]{1,0:T(8,128)(2,1)S(1)}, u32[]{:S(2)}, u32[]{:S(2)}) %collective-permute-start.1) | collective-permute-done | bytes 49184 | tf_op jit(solution)/shard_map/ppermute | solution.py:27
  14.4 0.1 collective-permute-done.2
  14.5 0.0 collective-permute-done.3.refs_1_.second_ref
  14.5 0.0 copy-start.8
  14.5 1.3 %broadcast_in_dim.50 = bf16[8,4,8,3072]{3,2,1,0:T(8,128)(2,1)} broadcast(bf16[4,8,3072]{2,1,0:T(8,128)(2,1)S(1)} %shard_map.58), dimensions={1,2,3} | broadcast | bytes 1769472 | tf_op jit(solution)/shard_map/broadcast_in_dim | solution.py:17
  15.9 5.9 %all-to-all-start = ((bf16[8,4,8,3072]{3,2,1,0:T(8,128)(2,1)}), bf16[8,4,8,3072]{3,2,1,0:T(8,128)(2,1)S(1)}, u32[]{:S(2)}, u32[]{:S(2)}) async-start(bf16[8,4,8,3072]{3,2,1,0:T(8,128)(2,1)} %broadcast_in_dim.50), calls=%async_computation | async-start | bytes 3145728 | tf_op jit(solution)/shard_map/all_to_all | solution.py:16
  21.8 0.1 reshape.103
  21.9 0.1 eq.13
  22.0 4.6 %fusion.5 = f32[256,3072]{1,0:T(8,128)S(1)} fusion(bf16[3072,1024]{1,0:T(8,128)(2,1)} %first_ref.1, s32[1024]{0:T(1024)S(1)} %get-tuple-element.28, s32[256]{0:T(256)S(1)} %eq.13), kind=kOutput, calls=%fused_computation.13 | convolution fusion | flops 1610874880 | bytes 9442304 | tf_op jit(solution)/shard_map/dot_general | solution.py:72
  26.7 5.8 %fusion = bf16[256,3072]{1,0:T(8,128)(2,1)} fusion(f32[256,3072]{1,0:T(8,128)S(1)} %fusion.5, bf16[3072,1024]{1,0:T(8,128)(2,1)} %collective-permute-done.3.refs_1_.second_ref, s32[1024]{0:T(1024)S(1)} %get-tuple-element.27, s32[256]{0:T(256)S(1)} %eq.13), kind=kOutput, calls=%fused_computation.2 | convolution fusion | flops 1612447744 | bytes 11015168 | tf_op jit(solution)/shard_map/dot_general | solution.py:72
  32.5 9.5 %all-to-all-done = bf16[8,4,8,3072]{3,2,1,0:T(8,128)(2,1)S(1)} async-done(((bf16[8,4,8,3072]{3,2,1,0:T(8,128)(2,1)}), bf16[8,4,8,3072]{3,2,1,0:T(8,128)(2,1)S(1)}, u32[]{:S(2)}, u32[]{:S(2)}) %all-to-all-start) | async-done | bytes 1572896 | tf_op jit(solution)/shard_map/all_to_all | solution.py:16
  42.0 1.1 copy-done.4
  43.1 5.2 %fusion.31 = (f32[256]{0:T(256)S(1)}, f32[256,1024]{1,0:T(8,128)S(1)}) fusion(bf16[256,3072]{1,0:T(8,128)(2,1)} %bitcast.54, bf16[3072,1024]{1,0:T(8,128)(2,1)} %first_ref.1), kind=kOutput, calls=%fused_computation.62 | convolution fusion | flops 1610874624 | bytes 8913920 | tf_op jit(solution)/shard_map/dot_general | solution.py:142
  48.4 5.1 %fusion.32 = (f32[256]{0:T(256)S(1)}, f32[256,1024]{1,0:T(8,128)S(1)}) fusion(bf16[256,3072]{1,0:T(8,128)(2,1)S(1)} %bitcast.56, bf16[3072,1024]{1,0:T(8,128)(2,1)} %collective-permute-done.3.refs_1_.second_ref), kind=kOutput, calls=%fused_computation.63 | convolution fusion | flops 1610874624 | bytes 8913920 | tf_op jit(solution)/shard_map/dot_general | solution.py:142
  53.5 0.7 exponential_reduce_fusion.1
  54.2 0.7 broadcast_in_dim.52
  54.9 6.5 %all-to-all-start.1 = ((f32[32,3,256]{2,1,0:T(4,128)}), f32[32,3,256]{2,1,0:T(4,128)S(1)}, u32[]{:S(2)}, u32[]{:S(2)}) async-start(f32[32,3,256]{2,1,0:T(4,128)} %broadcast_in_dim.52), calls=%async_computation.1 | async-start | bytes 262144 | tf_op jit(solution)/shard_map/all_to_all | solution.py:16
  61.4 0.5 fusion.12
  61.9 6.1 %shard_map.60.refs_1_ = f32[256,3072]{1,0:T(8,128)S(1)} custom-call(bf16[256,1024]{1,0:T(8,128)(2,1)S(1)} %get-tuple-element.22.first_g, bf16[256,1024]{1,0:T(8,128)(2,1)S(1)} %get-tuple-element.21.second_g, bf16[3072,1024]{1,0:T(8,128)(2,1)} %first_ref.1, bf16[3072,1024]{1,0:T(8,128)(2,1)} %collective-permute-done.3.refs_1_.second_ref), custom_call_target="tpu_custom_call" | custom-call | flops 3221225472 | bytes 12582912 | tf_op jit(solution)/shard_map/pallas_call | solution.py:105
  68.0 3.7 %all-to-all-done.1.refs_0_ = f32[32,3,256]{2,1,0:T(4,128)S(1)} async-done(((f32[32,3,256]{2,1,0:T(4,128)}), f32[32,3,256]{2,1,0:T(4,128)S(1)}, u32[]{:S(2)}, u32[]{:S(2)}) %all-to-all-start.1) | async-done | bytes 98336 | tf_op jit(solution)/shard_map/all_to_all | solution.py:16
  71.7 0.1 slice_reduce_fusion.1
  71.8 0.6 fusion.29
  72.4 0.7 copy-done.7
  73.1 1.8 %add_convert_fusion = bf16[256,3072]{1,0:T(8,128)(2,1)} fusion(bf16[256,3072]{1,0:T(8,128)(2,1)S(1)} %copy-done.7, f32[256,3072]{1,0:T(8,128)S(1)} %shard_map.60.refs_1_, f32[256]{0:T(256)S(1)} %get-tuple-element.18, f32[256]{0:T(256)S(1)} %get-tuple-element.20), kind=kLoop, calls=%fused_computation.7 | loop fusion | flops 3932160 | bytes 6293504 | tf_op jit(solution)/shard_map/convert_element_type | solution.py:162
  75.0 4.4 %all-to-all-start.2 = ((bf16[8,4,8,3072]{3,2,1,0:T(8,128)(2,1)}), bf16[8,4,8,3072]{3,2,1,0:T(8,128)(2,1)}, u32[]{:S(2)}, u32[]{:S(2)}) async-start(bf16[8,4,8,3072]{3,2,1,0:T(8,128)(2,1)} %bitcast.53), calls=%async_computation.2 | async-start | bytes 3145728 | tf_op jit(solution)/shard_map/all_to_all | solution.py:163
  79.4 0.0 copy-start.6
  79.4 0.1 collective-permute-start.5
  79.5 0.6 fusion.10
  80.2 0.6 collective-permute-start.6
  80.7 0.1 collective-permute-start.4
  80.8 2.1 %collective-permute-done.4 = f32[1,1]{1,0:T(1,128)} collective-permute-done((f32[1,1]{1,0:T(1,128)}, f32[1,1]{1,0:T(1,128)}, u32[]{:S(2)}, u32[]{:S(2)}) %collective-permute-start.4) | collective-permute-done | bytes 36 | tf_op jit(solution)/shard_map/ppermute | solution.py:50
  84.3 0.0 collective-permute-done.6
  84.3 5.4 %convolution_convert_fusion.refs_1_ = bf16[3072,1024]{1,0:T(8,128)(2,1)} fusion(bf16[256,3072]{1,0:T(8,128)(2,1)S(1)} %collective-permute-done.5, bf16[256,3072]{1,0:T(8,128)(2,1)S(1)} %bitcast.57, bf16[256,1024]{1,0:T(8,128)(2,1)S(1)} %collective-permute-done.6, bf16[256,1024]{1,0:T(8,128)(2,1)S(1)} %get-tuple-element.16), kind=kOutput, calls=%fused_computation | convolution fusion | flops 3232759808 | bytes 10485760 | tf_op jit(solution)/shard_map/dot_general | solution.py:172
  89.7 8.7 %all-to-all-done.2 = bf16[8,4,8,3072]{3,2,1,0:T(8,128)(2,1)} async-done(((bf16[8,4,8,3072]{3,2,1,0:T(8,128)(2,1)}), bf16[8,4,8,3072]{3,2,1,0:T(8,128)(2,1)}, u32[]{:S(2)}, u32[]{:S(2)}) %all-to-all-start.2) | async-done | bytes 1572896 | tf_op jit(solution)/shard_map/all_to_all | solution.py:163
  98.5 1.7 %convert_reduce_fusion.refs_0_ = f32[4,8,3072]{2,1,0:T(8,128)S(1)} fusion(bf16[8,4,8,3072]{3,2,1,0:T(8,128)(2,1)} %all-to-all-done.2), kind=kLoop, calls=%fused_computation.6 | loop fusion | flops 1474560 | bytes 1966080 | tf_op jit(solution)/shard_map/reduce_sum | solution.py:164
  100.2 2.9 %collective-permute-start.7 = (f32[8,3072]{1,0:T(8,128)S(1)}, f32[8,3072]{1,0:T(8,128)S(1)}, u32[]{:S(2)}, u32[]{:S(2)}) collective-permute-start(f32[8,3072]{1,0:T(8,128)S(1)} %get-tuple-element.11), channel_id=1, source_target_pairs={{0,32},{16,48},{32,0},{48,16},{1,33},{17,49},{33,1},{49,17},{2,34}... | collective-permute-start | bytes 294920 | tf_op jit(solution)/shard_map/ppermute | solution.py:27
  103.0 0.6 collective-permute-start.9
  103.7 3.5 %collective-permute-start.8 = (f32[8,3072]{1,0:T(8,128)S(1)}, f32[8,3072]{1,0:T(8,128)S(1)}, u32[]{:S(2)}, u32[]{:S(2)}) collective-permute-start(f32[8,3072]{1,0:T(8,128)S(1)} %get-tuple-element.13), channel_id=1, source_target_pairs={{0,48},{16,0},{32,16},{48,32},{1,49},{17,1},{33,17},{49,33},{2,50}... | collective-permute-start | bytes 294920 | tf_op jit(solution)/shard_map/ppermute | solution.py:27
  107.2 4.2 %collective-permute-done.7 = f32[8,3072]{1,0:T(8,128)S(1)} collective-permute-done((f32[8,3072]{1,0:T(8,128)S(1)}, f32[8,3072]{1,0:T(8,128)S(1)}, u32[]{:S(2)}, u32[]{:S(2)}) %collective-permute-start.7) | collective-permute-done | bytes 98336 | tf_op jit(solution)/shard_map/ppermute | solution.py:27
  111.4 0.4 collective-permute-done.9
  111.8 1.7 %collective-permute-done.8 = f32[8,3072]{1,0:T(8,128)S(1)} collective-permute-done((f32[8,3072]{1,0:T(8,128)S(1)}, f32[8,3072]{1,0:T(8,128)S(1)}, u32[]{:S(2)}, u32[]{:S(2)}) %collective-permute-start.8) | collective-permute-done | bytes 98336 | tf_op jit(solution)/shard_map/ppermute | solution.py:27
  113.5 0.6 fusion.24
  (34 shorter events, 0.2 us)
Async XLA Ops:
  0.6 13.9 %collective-permute-start.3 = (bf16[3072,1024]{1,0:T(8,128)(2,1)}, bf16[3072,1024]{1,0:T(8,128)(2,1)}, u32[]{:S(2)}, u32[]{:S(2)}) collective-permute-start(bf16[3072,1024]{1,0:T(8,128)(2,1)} %first_ref.1), channel_id=1, source_target_pairs={{0,1},{1,0},{2,3},{3,2},{4,5},{5,4},{6,7},{7,6},{8,9},{9,8},{10,11... | collective-permute-start | bytes 18874376 | tf_op jit(solution)/shard_map/ppermute | solution.py:50
  0.7 11.0 %collective-permute-start = (bf16[8,3072]{1,0:T(8,128)(2,1)}, bf16[8,3072]{1,0:T(8,128)(2,1)S(1)}, u32[]{:S(2)}, u32[]{:S(2)}) collective-permute-start(bf16[8,3072]{1,0:T(8,128)(2,1)} %param.3), channel_id=1, source_target_pairs={{0,32},{16,48},{32,0},{48,16},{1,33},{17,49},{33,1},{49,17},{2,34}... | collective-permute-start | bytes 147464 | tf_op jit(solution)/shard_map/ppermute | solution.py:27
  8.0 6.5 %collective-permute-start.2 = (bf16[8,3072]{1,0:T(8,128)(2,1)}, bf16[8,3072]{1,0:T(8,128)(2,1)S(1)}, u32[]{:S(2)}, u32[]{:S(2)}) collective-permute-start(bf16[8,3072]{1,0:T(8,128)(2,1)} %param.3), channel_id=1, source_target_pairs={{0,48},{16,0},{32,16},{48,32},{1,49},{17,1},{33,17},{49,33},{2,50}... | collective-permute-start | bytes 147464 | tf_op jit(solution)/shard_map/ppermute | solution.py:27
  8.0 6.4 %collective-permute-start.1 = (bf16[8,3072]{1,0:T(8,128)(2,1)}, bf16[8,3072]{1,0:T(8,128)(2,1)S(1)}, u32[]{:S(2)}, u32[]{:S(2)}) collective-permute-start(bf16[8,3072]{1,0:T(8,128)(2,1)} %param.3), channel_id=1, source_target_pairs={{0,16},{16,32},{32,48},{48,0},{1,17},{17,33},{33,49},{49,1},{2,18}... | collective-permute-start | bytes 147464 | tf_op jit(solution)/shard_map/ppermute | solution.py:27
  14.5 7.2 %copy-start.8 = (s32[512]{0:T(512)S(1)}, s32[512]{0:T(512)}, u32[]{:S(2)}) copy-start(s32[512]{0:T(512)} %param.5) | copy-start | bytes 6148
  15.9 26.1 %all-to-all-start = ((bf16[8,4,8,3072]{3,2,1,0:T(8,128)(2,1)}), bf16[8,4,8,3072]{3,2,1,0:T(8,128)(2,1)S(1)}, u32[]{:S(2)}, u32[]{:S(2)}) async-start(bf16[8,4,8,3072]{3,2,1,0:T(8,128)(2,1)} %broadcast_in_dim.50), calls=%async_computation | async-start | bytes 3145728 | tf_op jit(solution)/shard_map/all_to_all | solution.py:16
  42.0 1.1 copy-start.4
  43.1 5.2 %copy-start.5 = (bf16[8,4,8,3072]{3,2,1,0:T(8,128)(2,1)S(1)}, bf16[8,4,8,3072]{3,2,1,0:T(8,128)(2,1)}, u32[]{:S(2)}) copy-start(bf16[8,4,8,3072]{3,2,1,0:T(8,128)(2,1)} %copy-done.4) | copy-start | bytes 4718596
  48.4 13.0 %copy-start = (f32[256,1024]{1,0:T(8,128)}, f32[256,1024]{1,0:T(8,128)S(1)}, u32[]{:S(2)}) copy-start(f32[256,1024]{1,0:T(8,128)S(1)} %get-tuple-element.24) | copy-start | bytes 3145732
  53.5 8.4 %copy-start.2 = (f32[256,1024]{1,0:T(8,128)}, f32[256,1024]{1,0:T(8,128)S(1)}, u32[]{:S(2)}) copy-start(f32[256,1024]{1,0:T(8,128)S(1)} %get-tuple-element.26) | copy-start | bytes 3145732
  54.9 16.9 %all-to-all-start.1 = ((f32[32,3,256]{2,1,0:T(4,128)}), f32[32,3,256]{2,1,0:T(4,128)S(1)}, u32[]{:S(2)}, u32[]{:S(2)}) async-start(f32[32,3,256]{2,1,0:T(4,128)} %broadcast_in_dim.52), calls=%async_computation.1 | async-start | bytes 262144 | tf_op jit(solution)/shard_map/all_to_all | solution.py:16
  71.7 1.4 %copy-start.7 = (bf16[256,3072]{1,0:T(8,128)(2,1)S(1)}, bf16[256,3072]{1,0:T(8,128)(2,1)}, u32[]{:S(2)}) copy-start(bf16[256,3072]{1,0:T(8,128)(2,1)} %fusion) | copy-start | bytes 4718596
  75.0 4.5 %copy-start.1 = (f32[256,1024]{1,0:T(8,128)S(1)}, f32[256,1024]{1,0:T(8,128)}, u32[]{:S(2)}) copy-start(f32[256,1024]{1,0:T(8,128)} %copy-done) | copy-start | bytes 3145732
  75.0 4.5 %copy-start.3 = (f32[256,1024]{1,0:T(8,128)S(1)}, f32[256,1024]{1,0:T(8,128)}, u32[]{:S(2)}) copy-start(f32[256,1024]{1,0:T(8,128)} %copy-done.2) | copy-start | bytes 3145732
  75.0 23.5 %all-to-all-start.2 = ((bf16[8,4,8,3072]{3,2,1,0:T(8,128)(2,1)}), bf16[8,4,8,3072]{3,2,1,0:T(8,128)(2,1)}, u32[]{:S(2)}, u32[]{:S(2)}) async-start(bf16[8,4,8,3072]{3,2,1,0:T(8,128)(2,1)} %bitcast.53), calls=%async_computation.2 | async-start | bytes 3145728 | tf_op jit(solution)/shard_map/all_to_all | solution.py:163
  79.4 5.0 %copy-start.6 = (bf16[8,4,8,3072]{3,2,1,0:T(8,128)(2,1)S(1)}, bf16[8,4,8,3072]{3,2,1,0:T(8,128)(2,1)}, u32[]{:S(2)}) copy-start(bf16[8,4,8,3072]{3,2,1,0:T(8,128)(2,1)} %copy-done.4) | copy-start | bytes 4718596
  79.4 4.9 %collective-permute-start.5 = (bf16[256,3072]{1,0:T(8,128)(2,1)}, bf16[256,3072]{1,0:T(8,128)(2,1)S(1)}, u32[]{:S(2)}, u32[]{:S(2)}) collective-permute-start(bf16[256,3072]{1,0:T(8,128)(2,1)} %bitcast.55), channel_id=1, source_target_pairs={{0,1},{1,0},{2,3},{3,2},{4,5},{5,4},{6,7},{7,6},{8,9},{9,8},{10,11... | collective-permute-start | bytes 4718600 | tf_op jit(solution)/shard_map/ppermute | solution.py:50
  80.2 4.2 %collective-permute-start.6 = (bf16[256,1024]{1,0:T(8,128)(2,1)S(1)}, bf16[256,1024]{1,0:T(8,128)(2,1)S(1)}, u32[]{:S(2)}, u32[]{:S(2)}) collective-permute-start(bf16[256,1024]{1,0:T(8,128)(2,1)S(1)} %get-tuple-element.17), channel_id=1, source_target_pairs={{0,1},{1,0},{2,3},{3,2},{4,5},{5,4},{6,7},{7,6},{8,9},{9,8},{10,11... | collective-permute-start | bytes 1572872 | tf_op jit(solution)/shard_map/ppermute | solution.py:50
  80.7 2.2 %collective-permute-start.4 = (f32[1,1]{1,0:T(1,128)}, f32[1,1]{1,0:T(1,128)}, u32[]{:S(2)}, u32[]{:S(2)}) collective-permute-start(f32[1,1]{1,0:T(1,128)} %bitcast.12), channel_id=1, source_target_pairs={{0,1},{1,0},{2,3},{3,2},{4,5},{5,4},{6,7},{7,6},{8,9},{9,8},{10,11... | collective-permute-start | bytes 20 | tf_op jit(solution)/shard_map/ppermute | solution.py:50
  100.2 11.2 %collective-permute-start.7 = (f32[8,3072]{1,0:T(8,128)S(1)}, f32[8,3072]{1,0:T(8,128)S(1)}, u32[]{:S(2)}, u32[]{:S(2)}) collective-permute-start(f32[8,3072]{1,0:T(8,128)S(1)} %get-tuple-element.11), channel_id=1, source_target_pairs={{0,32},{16,48},{32,0},{48,16},{1,33},{17,49},{33,1},{49,17},{2,34}... | collective-permute-start | bytes 294920 | tf_op jit(solution)/shard_map/ppermute | solution.py:27
  103.0 8.8 %collective-permute-start.9 = (f32[8,3072]{1,0:T(8,128)S(1)}, f32[8,3072]{1,0:T(8,128)S(1)}, u32[]{:S(2)}, u32[]{:S(2)}) collective-permute-start(f32[8,3072]{1,0:T(8,128)S(1)} %get-tuple-element.12), channel_id=1, source_target_pairs={{0,16},{16,32},{32,48},{48,0},{1,17},{17,33},{33,49},{49,1},{2,18}... | collective-permute-start | bytes 294920 | tf_op jit(solution)/shard_map/ppermute | solution.py:27
  103.7 9.8 %collective-permute-start.8 = (f32[8,3072]{1,0:T(8,128)S(1)}, f32[8,3072]{1,0:T(8,128)S(1)}, u32[]{:S(2)}, u32[]{:S(2)}) collective-permute-start(f32[8,3072]{1,0:T(8,128)S(1)} %get-tuple-element.13), channel_id=1, source_target_pairs={{0,48},{16,0},{32,16},{48,32},{1,49},{17,1},{33,17},{49,33},{2,50}... | collective-permute-start | bytes 294920 | tf_op jit(solution)/shard_map/ppermute | solution.py:27
